TPU v7x, 32 devices: a whole 2x2x4 slice. The times are simulated.
32 devices in a mesh: dp: 8 (over y, x, core), tensor: 4 (over z).
Axes of the slice: x: 2, y: 2, z: 4, core: 2. Of those that a mesh axis runs over, the one named last changes fastest.
Arguments:
- x_rows: bfloat16 [64, 128, 3072], P('dp', 'tensor'), may hold values from -6 to 6
- g_rows: bfloat16 [64, 128, 3072], P('dp', 'tensor'), may hold values from -1.5 to 1.5
- w_up: bfloat16 [3072, 12288], P(None, 'tensor'), may hold values from -0.109375 to 0.109375
- w_down_t: bfloat16 [3072, 12288], P(None, 'tensor'), may hold values from -0.0546875 to 0.0546875
- block_count: int32 [8], replicated, may hold values from 1 to 8, 32 in all
- patches: int32 [8, 8], replicated, may hold values from 64 to 128, as said below
Outputs:
- input_grad: bfloat16 [32, 128, 3072], P('dp', 'tensor')
- up_grad: bfloat16 [3072, 12288], P('dp', 'tensor')
- down_grad_t: bfloat16 [3072, 12288], P('dp', 'tensor')
Inputs may be any that keep to these rules, and one draw needn't show every extreme that they name: `block_count`: the counts sum to 32; the largest is exactly 8. `patches`: in each source at least one block is full.
All inputs are finite; a program needn't handle non-finite values.
Results may differ from a plain program's by a relative error of at most 0.023.
Values may be sent and summed in bfloat16 or wider, within the bound.
No kernel may reach another device: no remote copies, remote signals or barrier semaphores. Data moves between devices by JAX's collectives and lax.ppermute only.
A program may use at most 192 MiB of HBM per device.

v0:
```python
import jax
import jax.numpy as jnp
from jax import lax
from jax.sharding import PartitionSpec as P

OWNB = 4


def gelu_pair(pre_act):
    normal_cdf = 0.5 * (1.0 + lax.erf(pre_act * 0.7071067811865476))
    density = jnp.exp(-0.5 * pre_act * pre_act) * 0.3989422804014327
    return (pre_act * normal_cdf, normal_cdf + pre_act * density)


def row_product(columns, hidden):
    return lax.dot_general(
        columns, hidden, (((0,), (0,)), ((), ())), preferred_element_type=jnp.float32
    )


def local(x_rows, g_rows, w_up, w_down_t, block_count, patches):
    dp_count = lax.axis_size("dp")
    dp_index = lax.axis_index("dp")
    tensor_index = lax.axis_index("tensor")
    block_total, rows_here, features = x_rows.shape
    starts = jnp.cumsum(block_count) - block_count
    block_ends = starts + block_count
    targets = jnp.arange(dp_count, dtype=jnp.int32)
    offsets = (targets - starts[dp_index]) % dp_count
    in_use = offsets < block_count[dp_index]
    picked = jnp.minimum(offsets, block_total - 1)
    filled = jnp.take(patches[dp_index], picked)
    row_index = tensor_index * rows_here + jnp.arange(rows_here, dtype=jnp.int32)
    row_keep = in_use[:, None] & (row_index[None, :] < filled[:, None])
    zero_value = jnp.zeros((), jnp.bfloat16)
    send_x = jnp.where(row_keep[:, :, None], jnp.take(x_rows, picked, axis=0), zero_value)
    send_g = jnp.where(row_keep[:, :, None], jnp.take(g_rows, picked, axis=0), zero_value)
    arrived_x, arrived_g = (
        lax.all_to_all(send_x, "dp", split_axis=0, concat_axis=0, tiled=True),
        lax.all_to_all(send_g, "dp", split_axis=0, concat_axis=0, tiled=True),
    )
    global_number = dp_index + dp_count * jnp.arange(OWNB, dtype=jnp.int32)
    source = jnp.sum((block_ends[None, :] <= global_number[:, None]).astype(jnp.int32), axis=1)
    piece_x = jnp.take(arrived_x, source, axis=0)
    piece_g = jnp.take(arrived_g, source, axis=0)
    owner_x, owner_g = (
        lax.all_gather(piece_x, "tensor", axis=1, tiled=True),
        lax.all_gather(piece_g, "tensor", axis=1, tiled=True),
    )
    flat_x = owner_x.reshape(-1, features)
    flat_g = owner_g.reshape(-1, features)
    pre_act = jnp.dot(flat_x, w_up, preferred_element_type=jnp.float32)
    gelu_value, gelu_slope = gelu_pair(pre_act)
    activation = gelu_value.astype(jnp.bfloat16)
    act_grad = jnp.dot(flat_g, w_down_t, preferred_element_type=jnp.float32)
    pre_grad = (act_grad * gelu_slope).astype(jnp.bfloat16)
    partial_value = lax.dot_general(
        pre_grad, w_up, (((1,), (1,)), ((), ())), preferred_element_type=jnp.float32
    )
    rounded = lax.optimization_barrier(partial_value.astype(jnp.bfloat16)).astype(jnp.float32)
    rounded = rounded.reshape(owner_x.shape[0], owner_x.shape[1], features)
    summed = lax.psum_scatter(
        rounded.astype(jnp.bfloat16), "tensor", scatter_dimension=1, tiled=True
    )
    columns = flat_x
    up_sum = lax.psum_scatter(
        row_product(columns, pre_grad).astype(jnp.bfloat16), "dp", scatter_dimension=0, tiled=True
    )
    columns = flat_g
    down_sum = lax.psum_scatter(
        row_product(columns, activation).astype(jnp.bfloat16), "dp", scatter_dimension=0, tiled=True
    )
    return (summed, up_sum, down_sum)


def solution(mesh):
    placed = (
        P("dp", "tensor", None),
        P("dp", "tensor", None),
        P(None, "tensor"),
        P(None, "tensor"),
        P(),
        P(),
    )
    return jax.shard_map(
        local,
        mesh=mesh,
        in_specs=placed,
        out_specs=(P("dp", "tensor", None), P("dp", "tensor"), P("dp", "tensor")),
        check_vma=False,
    )
```

profile of v0, /device:TPU:0, one launch (start us, length us, event | category | flops | bytes accessed | tf_op | source)
XLA Modules:
  0.0 559.1 jit_solution(16998740597948455637)
XLA Ops:
  7.2 0.0 copy-start
  7.2 0.9 reduce-window.8
  8.1 0.7 bitcast_subtract_fusion
  8.8 1.2 dynamic_slice.10
  10.0 0.6 dynamic_slice.9
  10.6 0.7 fusion.9
  11.3 0.7 dynamic-slice_bitcast_fusion
  12.0 0.6 gather_fusion
  12.6 0.7 compare_select_fusion.2
  13.3 1.3 compare_and_fusion.2
  14.6 0.0 copy-done
  14.6 0.6 gather_fusion.1
  15.3 2.1 gather_fusion.3
  17.4 0.1 compare_and_fusion
  17.4 1.6 select_select_fusion.1
  19.0 25.9 %all_to_all.10 = bf16[8,32,3072]{2,1,0:T(8,128)(2,1)S(1)} all-to-all(bf16[8,32,3072]{2,1,0:T(8,128)(2,1)S(1)} %get-tuple-element.6), channel_id=1, replica_groups=mesh['dp'=8,'tensor'=4] {'dp'}, dimensions={0} | all-to-all | bytes 3145728 | tf_op jit(solution)/shard_map/all_to_all | solution.py:39
  44.9 3.6 all-to-all-start
  48.5 0.0 all-gather.5.cloned.1.call-start
  48.6 0.2 convert_reduce_fusion
  48.8 1.5 gather_fusion.4
  50.3 19.2 %all-to-all-done = bf16[8,32,3072]{2,1,0:T(8,128)(2,1)S(1)} async-done(((bf16[8,32,3072]{2,1,0:T(8,128)(2,1)}), bf16[8,32,3072]{2,1,0:T(8,128)(2,1)S(1)}, u32[]{:S(2)}, u32[]{:S(2)}) %all-to-all-start) | async-done | bytes 1572896 | tf_op jit(solution)/shard_map/all_to_all | solution.py:40
  69.5 0.6 gather_fusion.2
  70.1 2.5 broadcast_select_fusion.1
  72.6 0.0 all-gather.5.cloned.1.call-update
  72.6 0.0 all-gather.3.cloned.1.call-start
  72.7 0.7 all-gather.3.cloned.1.call-update
  73.4 0.0 reduce-scatter.4.cloned.1.call-start
  73.4 62.2 %all-gather.5.cloned.1.call-done = bf16[4,128,3072]{2,1,0:T(8,128)(2,1)} async-done(((bf16[4,32,3072]{2,1,0:T(8,128)(2,1)}), bf16[4,128,3072]{2,1,0:T(8,128)(2,1)}) %all-gather.5.cloned.1.call-update) | async-done | bytes 3145744 | tf_op jit(solution)/shard_map/all_gather | solution.py:47
  135.6 16.3 %fusion.10 = f32[512,3072]{1,0:T(8,128)} fusion(bf16[512,3072]{1,0:T(8,128)(2,1)} %bitcast.22, bf16[3072,3072]{1,0:T(8,128)(2,1)} %param.12), kind=kOutput, calls=%fused_computation.47 | convolution fusion | flops 9663676416 | bytes 28311552 | tf_op jit(solution)/shard_map/dot_general | solution.py:52
  152.0 48.0 %all-gather.3.cloned.1.call-done = bf16[4,128,3072]{2,1,0:T(8,128)(2,1)} async-done(((bf16[4,32,3072]{2,1,0:T(8,128)(2,1)}), bf16[4,128,3072]{2,1,0:T(8,128)(2,1)}) %all-gather.3.cloned.1.call-update) | async-done | bytes 3145744 | tf_op jit(solution)/shard_map/all_gather | solution.py:48
  199.9 16.8 %fusion.5 = bf16[512,3072]{1,0:T(8,128)(2,1)S(1)} fusion(f32[512,3072]{1,0:T(8,128)} %fusion.10, bf16[512,3072]{1,0:T(8,128)(2,1)} %bitcast.24, bf16[3072,3072]{1,0:T(8,128)(2,1)} %param.13), kind=kOutput, calls=%fused_computation.13 | convolution fusion | flops 9679405056 | bytes 31457280 | tf_op jit(solution)/shard_map/dot_general | solution.py:55
  216.7 0.0 copy-start.2
  216.7 16.2 %convolution_convert_fusion.2 = bf16[512,3072]{1,0:T(8,128)(2,1)} fusion(bf16[512,3072]{1,0:T(8,128)(2,1)S(1)} %fusion.5, bf16[3072,3072]{1,0:T(8,128)(2,1)} %param.12), kind=kOutput, calls=%fused_computation.16 | convolution fusion | flops 9665249280 | bytes 25165824 | tf_op jit(solution)/shard_map/dot_general | solution.py:57
  233.0 0.0 copy-done.2
  233.0 0.0 reduce-scatter.4.cloned.1.call-update
  233.0 0.2 reduce-scatter.8.cloned.1.call-start
  233.2 17.1 %convolution_convert_fusion = bf16[3072,3072]{1,0:T(8,128)(2,1)} fusion(bf16[512,3072]{1,0:T(8,128)(2,1)} %bitcast.25, f32[512,3072]{1,0:T(8,128)} %fusion.10), kind=kOutput, calls=%fused_computation.5 | convolution fusion | flops 9680977920 | bytes 28311552 | tf_op jit(solution)/shard_map/dot_general | solution.py:16
  250.3 0.0 reduce-scatter.8.cloned.1.call-update
  250.4 0.0 reduce-scatter.6.cloned.1.call-start
  250.4 16.3 %convolution_convert_fusion.1 = bf16[3072,3072]{1,0:T(8,128)(2,1)} fusion(bf16[512,3072]{1,0:T(8,128)(2,1)} %bitcast.23, bf16[512,3072]{1,0:T(8,128)(2,1)} %copy-done.2), kind=kOutput, calls=%fused_computation.6 | convolution fusion | flops 9673113600 | bytes 25165824 | tf_op jit(solution)/shard_map/dot_general | solution.py:16
  266.7 0.0 reduce-scatter.6.cloned.1.call-update
  266.7 0.0 copy-start.1
  266.7 25.4 %reduce-scatter.4.cloned.1.call-done = bf16[4,32,3072]{2,1,0:T(8,128)(2,1)} async-done(((bf16[4,128,3072]{2,1,0:T(8,128)(2,1)}), bf16[4,32,3072]{2,1,0:T(8,128)(2,1)}) %reduce-scatter.4.cloned.1.call-update) | async-done | bytes 786448 | tf_op jit(solution)/shard_map/reduce_scatter | solution.py:62
  292.1 130.2 %reduce-scatter.8.cloned.1.call-done = bf16[384,3072]{1,0:T(8,128)(2,1)} async-done(((bf16[3072,3072]{1,0:T(8,128)(2,1)}), bf16[384,3072]{1,0:T(8,128)(2,1)}) %reduce-scatter.8.cloned.1.call-update) | async-done | bytes 2359312 | tf_op jit(solution)/shard_map/reduce_scatter | solution.py:70
  422.3 130.2 %reduce-scatter.6.cloned.1.call-done = bf16[384,3072]{1,0:T(8,128)(2,1)} async-done(((bf16[3072,3072]{1,0:T(8,128)(2,1)}), bf16[384,3072]{1,0:T(8,128)(2,1)}) %reduce-scatter.6.cloned.1.call-update) | async-done | bytes 2359312 | tf_op jit(solution)/shard_map/reduce_scatter | solution.py:66
  552.5 0.0 copy-done.1
  (7 shorter events, 0.0 us)
Async XLA Ops:
  7.2 7.5 %copy-start = (bf16[8,32,3072]{2,1,0:T(8,128)(2,1)S(1)}, bf16[8,32,3072]{2,1,0:T(8,128)(2,1)}, u32[]{:S(2)}) copy-start(bf16[8,32,3072]{2,1,0:T(8,128)(2,1)} %param.11) | copy-start | bytes 4718596
  44.9 24.5 %all-to-all-start = ((bf16[8,32,3072]{2,1,0:T(8,128)(2,1)}), bf16[8,32,3072]{2,1,0:T(8,128)(2,1)S(1)}, u32[]{:S(2)}, u32[]{:S(2)}) async-start(bf16[8,32,3072]{2,1,0:T(8,128)(2,1)} %get-tuple-element.5), calls=%async_computation | async-start | bytes 3145728 | tf_op jit(solution)/shard_map/all_to_all | solution.py:40
  48.5 87.1 %all-gather.5.cloned.1.call-start = ((), (), s32[]{:S(2)}) async-start(), calls=%async_computation.6 | async-start | bytes 3932160 | tf_op jit(solution)/shard_map/all_gather | solution.py:47
  72.6 127.3 %all-gather.3.cloned.1.call-start = ((), (), s32[]{:S(2)}) async-start(), calls=%async_computation.5 | async-start | bytes 3932160 | tf_op jit(solution)/shard_map/all_gather | solution.py:48
  73.4 218.8 %reduce-scatter.4.cloned.1.call-start = ((), (), s32[]{:S(2)}) async-start(), calls=%async_computation.7 | async-start | bytes 3932160 | tf_op jit(solution)/shard_map/reduce_scatter | solution.py:62
  216.7 16.3 %copy-start.2 = (bf16[512,3072]{1,0:T(8,128)(2,1)}, bf16[512,3072]{1,0:T(8,128)(2,1)S(1)}, u32[]{:S(2)}) copy-start(bf16[512,3072]{1,0:T(8,128)(2,1)S(1)} %fusion.5) | copy-start | bytes 9437188
  233.0 189.3 %reduce-scatter.8.cloned.1.call-start = ((), (), s32[]{:S(2)}) async-start(), calls=%async_computation.9 | async-start | bytes 21233664 | tf_op jit(solution)/shard_map/reduce_scatter | solution.py:70
  250.4 302.2 %reduce-scatter.6.cloned.1.call-start = ((), (), s32[]{:S(2)}) async-start(), calls=%async_computation.8 | async-start | bytes 21233664 | tf_op jit(solution)/shard_map/reduce_scatter | solution.py:66
  266.7 285.8 %copy-start.1 = (bf16[8,32,3072]{2,1,0:T(8,128)(2,1)S(1)}, bf16[8,32,3072]{2,1,0:T(8,128)(2,1)}, u32[]{:S(2)}) copy-start(bf16[8,32,3072]{2,1,0:T(8,128)(2,1)} %param.11) | copy-start | bytes 4718596
Sparse Core Ops, SparseCore 0:
  72.7 62.8 all-gather.4
  137.8 62.1 all-gather.2
  233.1 58.9 reduce-scatter.3
  296.2 126.1 reduce-scatter.7
  426.4 126.1 reduce-scatter.5
where the time goes:
time: 559 us
  waiting for transfers between devices  416 us (74%)
  matrix products  82.7 us (15%)
  blocking collectives  25.9 us (5%)
  between operations  13.9 us (2%)
  other arithmetic  8.59 us (2%)
  local copies, waits for them, and re-layouts  7.96 us (1%)
    reduce_scatter x1, waiting for transfers between devices, local(): lax.psum_scatter(row_product(columns, pre_grad).astype(jnp.bfloat16), 'dp...  130 us
    reduce_scatter x1, waiting for transfers between devices, local(): lax.psum_scatter(row_product(columns, activation).astype(jnp.bfloat16), '...  130 us
    all_gather x1, waiting for transfers between devices, local(): lax.all_gather(piece_x, 'tensor', axis=1, tiled=True)  62.2 us
    all_gather x1, waiting for transfers between devices, local(): lax.all_gather(piece_g, 'tensor', axis=1, tiled=True)  48 us
    dot_general x2, matrix products, row_product(): lax.dot_general(columns, hidden, (((0,), (0,)), ((), ())), preferred_elem...  33.4 us
    all_to_all x1, blocking collectives, local(): lax.all_to_all(send_x, 'dp', split_axis=0, concat_axis=0, tiled=True)  25.9 us
    reduce_scatter x1, waiting for transfers between devices, local(): lax.psum_scatter(rounded.astype(jnp.bfloat16), 'tensor', scatter_dimensio...  25.4 us
    all_to_all x1, waiting for transfers between devices, local(): lax.all_to_all(send_g, 'dp', split_axis=0, concat_axis=0, tiled=True)  19.2 us
  transfers between devices with their start and end apart: 6, of which 6 were waited for; matrix products, arithmetic and copies ran while one was open for 9% of the time, Pallas kernels for 0%

commit v1 on v0

v1 whole, which is shorter than its diff:
```python
import functools

import jax
import jax.numpy as jnp
from jax import lax
from jax.experimental import pallas as pl
from jax.experimental.pallas import tpu as pltpu
from jax.sharding import PartitionSpec as P

OWNB = 4
BF16 = jnp.bfloat16
F32 = jnp.float32
VMEM_LIMIT = 60 * 1024 * 1024
SHORT = pl.CostEstimate(flops=1, bytes_accessed=1, transcendentals=0)


def chip_with(j, v, core):
    return jnp.where(core == 0, 2 * j + v, ((j >> 1) << 2) + 2 * v + (j & 1))


def pool_bit(chip, core):
    return jnp.where(core == 0, chip & 1, (chip >> 1) & 1)


def other_bits(chip, core):
    return jnp.where(core == 0, chip >> 1, ((chip >> 2) << 1) + (chip & 1))


def chip_perm(dp, flip, cross=False):
    return [(i, 2 * ((i >> 1) ^ flip(i & 1)) + ((i & 1) ^ int(cross))) for i in range(dp)]


def start_of(count, source, dp):
    total = jnp.int32(0)
    for j in range(dp):
        total = total + jnp.where(source > j, count[j], 0)
    return total


def source_of(count, number, dp):
    end, source = jnp.int32(0), jnp.int32(0)
    for j in range(dp):
        end = end + count[j]
        source = source + jnp.where(end <= number, 1, 0)
    return source


def pack_body(info, count, x, g, x_out, g_out, sems):
    dp, blocks = x_out.shape[0], x.shape[0]
    start = start_of(count, info[0], dp)
    copies = []
    for t, (rows, out) in enumerate(((x, x_out), (g, g_out))):
        for k in range(dp):
            block = jnp.minimum(lax.rem(k + OWNB * dp - start, dp), blocks - 1)
            copies.append(pltpu.make_async_copy(rows.at[block], out.at[k], sems.at[t, k]))
    for copy in copies:
        copy.start()
    for copy in copies:
        copy.wait()


def pack(x_rows, g_rows, info, count, dp):
    _, here, d = x_rows.shape
    shape = jax.ShapeDtypeStruct((dp, here, d), BF16)
    any_spec = pl.BlockSpec(memory_space=pl.ANY)
    return pl.pallas_call(
        pack_body,
        out_shape=(shape, shape),
        grid_spec=pltpu.PrefetchScalarGridSpec(
            num_scalar_prefetch=2,
            in_specs=[any_spec, any_spec],
            out_specs=(any_spec, any_spec),
            scratch_shapes=[pltpu.SemaphoreType.DMA((2, dp))],
        ),
        compiler_params=pltpu.CompilerParams(vmem_limit_bytes=VMEM_LIMIT),
        cost_estimate=SHORT,
    )(info, count, x_rows, g_rows)


def select_body(info, count, patches, rows, out, *, dp):
    number = info[0] + dp * pl.program_id(0)
    source = source_of(count, number, dp)
    filled = patches[source, number - start_of(count, source, dp)]
    here = rows.shape[1]
    row = lax.broadcasted_iota(jnp.int32, rows.shape, 1) + info[1] * here
    out[...] = jnp.where(row < filled, rows[...].astype(F32), 0.0).astype(out.dtype)


def select(arrived, info, count, patches):
    dp, here, d = arrived.shape
    return pl.pallas_call(
        functools.partial(select_body, dp=dp),
        out_shape=jax.ShapeDtypeStruct((OWNB, here, d), arrived.dtype),
        grid_spec=pltpu.PrefetchScalarGridSpec(
            num_scalar_prefetch=3,
            grid=(OWNB,),
            in_specs=[pl.BlockSpec((1, here, d), lambda m, i, n, p: (source_of(n, i[0] + dp * m, dp), 0, 0))],
            out_specs=pl.BlockSpec((1, here, d), lambda m, i, n, p: (m, 0, 0)),
        ),
        compiler_params=pltpu.CompilerParams(vmem_limit_bytes=VMEM_LIMIT),
        cost_estimate=SHORT,
    )(info, count, patches, arrived)


def block_of(size, most):
    for width in range(most, 0, -128):
        if size % width == 0:
            return width
    return size


def load_rows(own, sib, rows):
    half = own.shape[0]
    rows[:half] = own[...]
    rows[half:] = sib[...]


def put_partner_columns(info, rows, out, hidden, chips):
    core, chip = info[0] & 1, info[0] >> 1
    width = rows.shape[1] // chips
    away = 1 - pool_bit(chip, core)
    for j in range(chips // 2):
        at = pl.multiple_of(chip_with(j, away, core) * width, 128)
        out[:, hidden + j * width:hidden + (j + 1) * width] = rows[:, pl.ds(at, width)]


def up_body(info, own, sib, w, out, slope, rows, *, hidden, chips):
    n = pl.program_id(0)

    @pl.when(n == 0)
    def _():
        load_rows(own, sib, rows)
        put_partner_columns(info, rows, out, hidden, chips)

    pre_act = jnp.dot(rows[...], w[...], preferred_element_type=F32)
    cdf = 0.5 * (1.0 + lax.erf(pre_act * 0.7071067811865476))
    density = jnp.exp(-0.5 * pre_act * pre_act) * 0.3989422804014327
    width = w.shape[1]
    out[:, pl.ds(pl.multiple_of(n * width, 128), width)] = (pre_act * cdf).astype(out.dtype)
    slope[...] = (cdf + pre_act * density).astype(slope.dtype)


def down_body(info, own, sib, w, slope, out, rows, *, hidden, chips):
    n = pl.program_id(0)

    @pl.when(n == 0)
    def _():
        load_rows(own, sib, rows)
        if out.shape[1] > hidden:
            put_partner_columns(info, rows, out, hidden, chips)

    act_grad = jnp.dot(rows[...], w[...], preferred_element_type=F32)
    width = w.shape[1]
    out[:, pl.ds(pl.multiple_of(n * width, 128), width)] = (act_grad * slope[...]).astype(out.dtype)


def columns_body(info, own, sib, out, rows, *, chips):
    load_rows(own, sib, rows)
    put_partner_columns(info, rows, out, 0, chips)


def partner_columns(own, sib, info, chips):
    half, d = own.shape
    spec = pl.BlockSpec((half, d), lambda n, i: (0, 0))
    return pl.pallas_call(
        functools.partial(columns_body, chips=chips),
        out_shape=jax.ShapeDtypeStruct((2 * half, d // 2), BF16),
        grid_spec=pltpu.PrefetchScalarGridSpec(
            num_scalar_prefetch=1,
            grid=(1,),
            in_specs=[spec, spec],
            out_specs=pl.BlockSpec((2 * half, d // 2), lambda n, i: (0, 0)),
            scratch_shapes=[pltpu.VMEM((2 * half, d), BF16)],
        ),
        compiler_params=pltpu.CompilerParams(vmem_limit_bytes=VMEM_LIMIT),
        cost_estimate=SHORT,
    )(info, own, sib)


def forward(own, sib, w, info, chips, slope=None, with_columns=True):
    half, d = own.shape
    hidden = w.shape[1] // 2
    width = block_of(hidden, 768)
    steps = hidden // width
    across = hidden + (d // 2 if with_columns else 0)
    out_shape = jax.ShapeDtypeStruct((2 * half, across), BF16)
    out_spec = pl.BlockSpec((2 * half, across), lambda n, i: (0, 0))
    slope_spec = pl.BlockSpec((2 * half, width), lambda n, i: (0, n))
    rows_spec = pl.BlockSpec((half, d), lambda n, i: (0, 0))
    w_spec = pl.BlockSpec((d, width), lambda n, i: (0, (i[0] & 1) * steps + n))
    in_specs = [rows_spec, rows_spec, w_spec]
    operands = [own, sib, w]
    if slope is None:
        body = up_body
        out_shape = (out_shape, jax.ShapeDtypeStruct((2 * half, hidden), BF16))
        out_specs = (out_spec, slope_spec)
    else:
        body = down_body
        out_specs = out_spec
        in_specs.append(slope_spec)
        operands.append(slope)
    return pl.pallas_call(
        functools.partial(body, hidden=hidden, chips=chips),
        out_shape=out_shape,
        grid_spec=pltpu.PrefetchScalarGridSpec(
            num_scalar_prefetch=1,
            grid=(steps,),
            in_specs=in_specs,
            out_specs=out_specs,
            scratch_shapes=[pltpu.VMEM((2 * half, d), BF16)],
        ),
        compiler_params=pltpu.CompilerParams(vmem_limit_bytes=VMEM_LIMIT),
        cost_estimate=SHORT,
    )(info, *operands)


def input_body(info, pre, w, own, sib):
    value = lax.dot_general(pre[...], w[...], (((1,), (1,)), ((), ())), preferred_element_type=F32)
    half = own.shape[0]
    own[...] = value[:half].astype(own.dtype)
    sib[...] = value[half:].astype(sib.dtype)


def input_part(pre, w, info):
    rows = pre.shape[0]
    d, hidden = w.shape[0], w.shape[1] // 2
    width = block_of(d, 768)
    shape = jax.ShapeDtypeStruct((rows // 2, d), BF16)
    spec = pl.BlockSpec((rows // 2, width), lambda n, i: (0, n))
    return pl.pallas_call(
        input_body,
        out_shape=(shape, shape),
        grid_spec=pltpu.PrefetchScalarGridSpec(
            num_scalar_prefetch=1,
            grid=(d // width,),
            in_specs=[
                pl.BlockSpec((rows, hidden), lambda n, i: (0, 0)),
                pl.BlockSpec((width, hidden), lambda n, i: (n, i[0] & 1)),
            ],
            out_specs=(spec, spec),
        ),
        compiler_params=pltpu.CompilerParams(vmem_limit_bytes=VMEM_LIMIT),
        cost_estimate=SHORT,
    )(info, pre, w)


def weight_body(at, *refs, slots):
    ins, (straight, crossed) = refs[:5 * slots], refs[5 * slots:]
    total = None
    dims = (((0,), (0,)), ((), ()))
    for s in range(slots):
        own, sib, there, mine, theirs = ins[5 * s:5 * s + 5]
        half = own.shape[0]
        for left, right in ((own[...], mine[:half]), (sib[...], mine[half:]), (there[...], theirs[...])):
            term = lax.dot_general(left, right, dims, preferred_element_type=F32)
            total = term if total is None else total + term
    span = straight.shape[0]
    low, high = total[:span], total[span:]
    first = at[2] == 0
    straight[...] = jnp.where(first, low, high).astype(straight.dtype)
    crossed[...] = jnp.where(first, high, low).astype(crossed.dtype)


def weight_part(rows, there_rows, rights, own_at, there_at, core, width, hidden):
    slots = len(rows)
    at = jnp.stack([own_at, there_at, core]).astype(jnp.int32)
    block = block_of(hidden, 512)
    operands, specs = [], []
    for (own, sib), (there, begin), (mine, theirs) in zip(rows, there_rows, rights):
        half = own.shape[0]
        operands += [own, sib, there, mine, theirs]
        specs += [
            pl.BlockSpec((half, width), lambda n, a: (0, a[0])),
            pl.BlockSpec((half, width), lambda n, a: (0, a[0])),
            pl.BlockSpec((2 * half, width), lambda n, a, first=begin // width: (0, first + a[1])),
            pl.BlockSpec((2 * half, block), lambda n, a: (0, n)),
            pl.BlockSpec((2 * half, block), lambda n, a: (0, n)),
        ]
    total = 4 * half * slots
    shape = jax.ShapeDtypeStruct((width // 2, hidden), BF16)
    spec = pl.BlockSpec((width // 2, block), lambda n, a: (0, n))
    return pl.pallas_call(
        functools.partial(weight_body, slots=slots),
        out_shape=(shape, shape),
        grid_spec=pltpu.PrefetchScalarGridSpec(
            num_scalar_prefetch=1,
            grid=(hidden // block,),
            in_specs=specs,
            out_specs=(spec, spec),
        ),
        compiler_params=pltpu.CompilerParams(vmem_limit_bytes=VMEM_LIMIT),
        cost_estimate=SHORT,
    )(at, *operands)


def add(*values):
    return sum(v.astype(F32) for v in values).astype(BF16)


def local(x_rows, g_rows, w_up, w_down_t, block_count, patches):
    dp, tensor = lax.axis_size("dp"), lax.axis_size("tensor")
    chips = dp // 2
    me, plane = lax.axis_index("dp"), lax.axis_index("tensor")
    chip, core = me >> 1, me & 1
    info = jnp.stack([me, plane]).astype(jnp.int32)
    here, d = x_rows.shape[1:]
    hidden = w_up.shape[1] // 2
    ring = [(i, (i + 1) % tensor) for i in range(tensor)]
    to_sibling = [(i, i ^ 1) for i in range(dp)]
    to_pool = chip_perm(dp, lambda c: 1 << c)
    last = []

    def after(*values):
        out = lax.optimization_barrier((*values, *last))[:len(values)]
        return out if len(out) > 1 else out[0]

    def done(value):
        last[:] = [value]
        return value

    def exchange(rows):
        return lax.all_to_all(rows, "dp", split_axis=0, concat_axis=0, tiled=True)

    def onward(piece):
        return lax.ppermute(piece, "tensor", ring)

    def sibling(piece):
        return lax.ppermute(piece, "dp", to_sibling)

    def pooled(piece):
        return lax.ppermute(piece, "dp", to_pool)

    def chosen(arrived):
        return done(select(after(arrived), info, block_count, patches)).reshape(OWNB * here, d)

    send_x, send_g = pack(x_rows, g_rows, info, block_count, dp)
    arrived_x = done(exchange(send_x))
    arrived_g = exchange(after(send_g))
    x_own = [chosen(arrived_x)]
    x_sib, g_own, g_sib = [sibling(x_own[0])], [], []
    x_ahead = onward(x_own[0])
    act, slope, pre, shares = [], [], [], []

    def up(s):
        mine, slope_s = forward(*after(x_own[s], x_sib[s]), w_up, info, chips)
        slope.append(slope_s)
        act.append((mine, pooled(done(mine))))

    def down(s, with_columns=True):
        mine = done(forward(*after(g_own[s], g_sib[s]), w_down_t, info, chips, slope[s], with_columns))
        pre.append((mine, pooled(mine)))

    def share(s):
        own, sib = input_part(after(pre[s][0]), w_up, info)
        shares.append((own, sibling(done(sib))))

    def arrive(own, sib, ahead, further=True):
        piece = after(ahead)
        own.append(piece)
        sib.append(sibling(piece))
        return onward(piece) if further else None

    def settle(pairs, s):
        if 0 <= s < len(pairs):
            last.append(pairs[s][1])

    up(0)
    for s in range(1, tensor):
        x_ahead = arrive(x_own, x_sib, x_ahead, s + 1 < tensor)
        if s == tensor - 1:
            g_ahead = onward(after(g_own[0]))
        settle(act, s - 2)
        up(s)
        if s == 1:
            g_own.append(chosen(arrived_g))
            g_sib.append(sibling(g_own[0]))
        if s == 2:
            settle(act, 1)
            down(0)
    settle(act, tensor - 2)
    share(0)
    g_last = None
    for s in range(1, tensor):
        g_ahead = arrive(g_own, g_sib, g_ahead, s + 1 < tensor)
        if s == tensor - 1:
            running = onward(add(*after(*shares[1])))
            g_last = partner_columns(*after(g_own[s], g_sib[s]), info, chips)
            g_last = pooled(done(g_last))
        settle(pre, s - 2 if s > 2 else -1)
        down(s, s < tensor - 1)
        settle(pre if s == 1 else act, 0 if s == 1 else tensor - 1 if s == 2 else -1)
        share(s)

    span = d // dp
    near, mine_j = pool_bit(chip, core), other_bits(chip, core)
    g_there = [(theirs, hidden) for _, theirs in pre[:-1]] + [(g_last, 0)]
    x_there = [(theirs, hidden) for _, theirs in act]
    sums = {"down": (list(zip(g_own, g_sib)), g_there, act), "up": (list(zip(x_own, x_sib)), x_there, pre)}

    def part(key, r):
        j = mine_j ^ r
        at = chip_with(j, near, core)
        straight, crossed = weight_part(*sums[key], at, j, core, 2 * span, hidden)
        return [straight, crossed]

    bits = (chips // 2).bit_length() - 1
    halves = {key: {} for key in sums}
    for key in sums:
        for r in reversed(range(1, chips // 2)):
            halves[key][r] = part(key, r)
    for s in range(2, tensor):
        running = onward(add(*shares[s], running))
    input_grad = add(*shares[0], running).reshape(OWNB, here, d)
    for key in sums:
        halves[key][0] = part(key, 0)

    def finished(parts):
        for k in reversed(range(1, bits)):
            perm = chip_perm(dp, lambda c: 2 << k)
            for r in range(1 << k, 2 << k):
                for h in range(2):
                    parts[r ^ (1 << k)][h] = add(parts[r ^ (1 << k)][h], lax.ppermute(parts[r][h], "dp", perm))
        flip = lambda c: 2 >> c
        straight = lax.ppermute(parts[1][0], "dp", chip_perm(dp, flip))
        crossed = lax.ppermute(parts[1][1], "dp", chip_perm(dp, flip, True))
        mine = add(parts[0][0], straight)
        other = add(sibling(parts[0][1]), crossed)
        return jnp.where(
            core == 0, jnp.concatenate([mine, other], axis=1), jnp.concatenate([other, mine], axis=1)
        )

    down_grad = finished(halves["down"])
    up_grad = finished(halves["up"])
    return input_grad, up_grad, down_grad


def solution(mesh):
    placed = (
        P("dp", "tensor", None),
        P("dp", "tensor", None),
        P(None, "tensor"),
        P(None, "tensor"),
        P(),
        P(),
    )
    return jax.shard_map(
        local,
        mesh=mesh,
        in_specs=placed,
        out_specs=(P("dp", "tensor", None), P("dp", "tensor"), P("dp", "tensor")),
        check_vma=False,
    )
```

time: 559 us -> 419 us (0.75)
  waiting for transfers between devices: 416 us -> 96.9 us
  Pallas kernels: 0 us -> 253 us
  matrix products: 82.7 us -> 0 us
  starting transfers between devices: 3.97 us -> 20.3 us
  between operations: 13.9 us -> 0.84 us
  other arithmetic: 8.59 us -> 16.5 us
    reduce_scatter x3 -> x0, waiting for transfers between devices: 286 us -> none  [the longest x1 130 us: local(): lax.psum_scatter(row_product(columns, pre_grad).astype(jnp.bfloat16), 'dp...]
    pallas_call x0 -> x20, Pallas kernels: none -> 253 us  [the longest x1 97.2 us: pack(): pl.pallas_call(pack_body, out_shape=(shape, shape), grid_spec=pltpu.Prefe...]
    all_gather x2 -> x0, waiting for transfers between devices: 110 us -> none  [the longest x1 62.2 us: local(): lax.all_gather(piece_x, 'tensor', axis=1, tiled=True)]
    ppermute x0 -> x36, waiting for transfers between devices: none -> 96.9 us  [the longest x9 44 us: onward(): return lax.ppermute(piece, 'tensor', ring)]
    dot_general x5 -> x0, matrix products: 82.7 us -> none  [the longest x2 33.4 us: row_product(): lax.dot_general(columns, hidden, (((0,), (0,)), ((), ())), preferred_elem...]
    all_to_all x1, waiting for transfers between devices: 19.2 us -> 0.01 us  [exchange(): return lax.all_to_all(rows, 'dp', split_axis=0, concat_axis=0, tiled=True)]
    ppermute x0 -> x36, starting transfers between devices: none -> 16 us  [the longest x9 5.34 us: pooled(): return lax.ppermute(piece, 'dp', to_pool)]
    convert_element_type x0 -> x8, other arithmetic: none -> 11.8 us  [add(): return sum((v.astype(F32) for v in values)).astype(BF16)]
  transfers between devices with their start and end apart: 6 -> 37, of which waited for: 6 -> 16; matrix products, arithmetic and copies ran while one was open for 9% -> 3% of each run, Pallas kernels for 0% -> 36%
where the time goes in v1:
time: 419 us; the launch traced here: 418 us
  Pallas kernels  253 us (60%)
  waiting for transfers between devices  96.9 us (23%)
  blocking collectives  26.3 us (6%)
  starting transfers between devices  20.3 us (5%)
  other arithmetic  16.5 us (4%)
  local copies, waits for them, and re-layouts  4.49 us (1%)
    pallas_call x1, Pallas kernels, pack(): pl.pallas_call(pack_body, out_shape=(shape, shape), grid_spec=pltpu.Prefe...  97.2 us
    pallas_call x8, Pallas kernels, forward(): pl.pallas_call(functools.partial(body, hidden=hidden, chips=chips), out_s...  63 us
    pallas_call x4, Pallas kernels, weight_part(): pl.pallas_call(functools.partial(weight_body, slots=slots), out_shape=(sh...  50.1 us
    ppermute x9, waiting for transfers between devices, onward(): return lax.ppermute(piece, 'tensor', ring)  44 us
    pallas_call x4, Pallas kernels, input_part(): pl.pallas_call(input_body, out_shape=(shape, shape), grid_spec=pltpu.Pref...  31.1 us
    all_to_all x1, blocking collectives, exchange(): return lax.all_to_all(rows, 'dp', split_axis=0, concat_axis=0, tiled=True)  26.3 us
    ppermute x9, waiting for transfers between devices, pooled(): return lax.ppermute(piece, 'dp', to_pool)  24.7 us
    convert_element_type x8, other arithmetic, add(): return sum((v.astype(F32) for v in values)).astype(BF16)  11.8 us
  transfers between devices with their start and end apart: 37, of which 16 were waited for; matrix products, arithmetic and copies ran while one was open for 3% of the time, Pallas kernels for 36%

profile of v1, /device:TPU:0, one launch (start us, length us, event | category | flops | bytes accessed | tf_op | source)
XLA Modules:
  0.0 418.0 jit_solution(7849396719949633052)
XLA Ops:
  1.3 97.2 %shard_map.85 = (bf16[8,32,3072]{2,1,0:T(8,128)(2,1)}, bf16[8,32,3072]{2,1,0:T(8,128)(2,1)}) custom-call(s32[2]{0:T(128)} %pad_add_fusion.info, s32[8]{0:T(128)} %count.5, bf16[8,32,3072]{2,1,0:T(8,128)(2,1)} %x.1, bf16[8,32,3072]{2,1,0:T(8,128)(2,1)} %g.1), custom_call_target="tpu_custom_call" | custom-call | flops 1 | bytes 1 | tf_op jit(solution)/shard_map/pallas_call | solution.py:66
  98.5 26.3 %all_to_all.10.rows = bf16[8,32,3072]{2,1,0:T(8,128)(2,1)} all-to-all(bf16[8,32,3072]{2,1,0:T(8,128)(2,1)} %get-tuple-element.64), channel_id=1, replica_groups=mesh['dp'=8,'tensor'=4] {'dp'}, dimensions={0} | all-to-all | bytes 3145728 | tf_op jit(solution)/shard_map/all_to_all | solution.py:322
  124.8 4.1 shard_map.86
  128.9 2.0 collective-permute-start
  130.9 4.3 %all-to-all-start.1 = ((bf16[8,32,3072]{2,1,0:T(8,128)(2,1)}), bf16[8,32,3072]{2,1,0:T(8,128)(2,1)}, u32[]{:S(2)}, u32[]{:S(2)}) async-start(bf16[8,32,3072]{2,1,0:T(8,128)(2,1)} %get-tuple-element.65), calls=%async_computation.1 | async-start | bytes 3145728 | tf_op jit(solution)/shard_map/all_to_all | solution.py:322
  136.1 8.0 %shard_map.87 = (bf16[256,3072]{1,0:T(8,128)(2,1)}, bf16[256,1536]{1,0:T(8,128)(2,1)}) custom-call(s32[2]{0:T(128)} %pad_add_fusion.info, bf16[128,3072]{1,0:T(8,128)(2,1)} %bitcast.12, bf16[128,3072]{1,0:T(8,128)(2,1)} %copy-done.9, bf16[3072,3072]{1,0:T(8,128)(2,1)} %w.23), custom_call_target="tpu_custom_call" | custom-call | flops 1 | bytes 1 | tf_op jit(solution)/shard_map/pallas_call | solution.py:202
  144.2 7.3 %collective-permute-done.own.refs_5_ = bf16[128,3072]{1,0:T(8,128)(2,1)} collective-permute-done((bf16[128,3072]{1,0:T(8,128)(2,1)}, bf16[128,3072]{1,0:T(8,128)(2,1)}, u32[]{:S(2)}, u32[]{:S(2)}) %collective-permute-start) | collective-permute-done | bytes 786464 | tf_op jit(solution)/shard_map/ppermute | solution.py:325
  152.1 1.9 collective-permute-done.2.sib.refs_6_
  154.9 8.1 %shard_map.88 = (bf16[256,3072]{1,0:T(8,128)(2,1)}, bf16[256,1536]{1,0:T(8,128)(2,1)}) custom-call(s32[2]{0:T(128)} %pad_add_fusion.info, bf16[128,3072]{1,0:T(8,128)(2,1)} %collective-permute-done.own.refs_5_, bf16[128,3072]{1,0:T(8,128)(2,1)} %copy-done.10, bf16[3072,3072]{1,0:T(8,128)(2,1)} %w.23), custom_call_target="tpu_custom_call" | custom-call | flops 1 | bytes 1 | tf_op jit(solution)/shard_map/pallas_call | solution.py:202
  163.5 4.1 shard_map.89
  167.6 5.9 %collective-permute-done.4.own.refs_10_ = bf16[128,3072]{1,0:T(8,128)(2,1)} collective-permute-done((bf16[128,3072]{1,0:T(8,128)(2,1)}, bf16[128,3072]{1,0:T(8,128)(2,1)}, u32[]{:S(2)}, u32[]{:S(2)}) %collective-permute-start.4) | collective-permute-done | bytes 786464 | tf_op jit(solution)/shard_map/ppermute | solution.py:325
  174.1 2.1 collective-permute-done.5.sib.refs_11_
  176.2 8.1 %shard_map.90 = (bf16[256,3072]{1,0:T(8,128)(2,1)}, bf16[256,1536]{1,0:T(8,128)(2,1)}) custom-call(s32[2]{0:T(128)} %pad_add_fusion.info, bf16[128,3072]{1,0:T(8,128)(2,1)} %collective-permute-done.4.own.refs_10_, bf16[128,3072]{1,0:T(8,128)(2,1)} %collective-permute-done.5.sib.refs_11_, bf16[3072,3072]{1,0:T(8,128)(2,1)} %w.23), custom_call_target="tpu_custom_call" | custom-call | flops 1 | bytes 1 | tf_op jit(solution)/shard_map/pallas_call | solution.py:202
  184.8 4.2 collective-permute-done.7.refs_7_.refs_9_
  189.0 7.7 %shard_map.91.pre.refs_3_ = bf16[256,3072]{1,0:T(8,128)(2,1)} custom-call(s32[2]{0:T(128)} %pad_add_fusion.info, bf16[128,3072]{1,0:T(8,128)(2,1)} %bitcast.16, bf16[128,3072]{1,0:T(8,128)(2,1)} %collective-permute-done.3.sib.refs_1_, bf16[3072,3072]{1,0:T(8,128)(2,1)} %w.22, bf16[256,1536]{1,0:T(8,128)(2,1)} %get-tuple-element.81.slope), custom_call_target="tpu_custom_call" | custom-call | flops 1 | bytes 1 | tf_op jit(solution)/shard_map/pallas_call | solution.py:202
  197.9 1.6 collective-permute-start.12
  200.9 8.1 %shard_map.92 = (bf16[256,3072]{1,0:T(8,128)(2,1)}, bf16[256,1536]{1,0:T(8,128)(2,1)}) custom-call(s32[2]{0:T(128)} %pad_add_fusion.info, bf16[128,3072]{1,0:T(8,128)(2,1)} %collective-permute-done.8.own.refs_15_, bf16[128,3072]{1,0:T(8,128)(2,1)} %copy-done.11, bf16[3072,3072]{1,0:T(8,128)(2,1)} %w.23), custom_call_target="tpu_custom_call" | custom-call | flops 1 | bytes 1 | tf_op jit(solution)/shard_map/pallas_call | solution.py:202
  209.0 7.7 %shard_map.93 = (bf16[128,3072]{1,0:T(8,128)(2,1)}, bf16[128,3072]{1,0:T(8,128)(2,1)}) custom-call(s32[2]{0:T(128)} %pad_add_fusion.info, bf16[256,3072]{1,0:T(8,128)(2,1)} %shard_map.91.pre.refs_3_, bf16[3072,3072]{1,0:T(8,128)(2,1)} %w.23), custom_call_target="tpu_custom_call" | custom-call | flops 1 | bytes 1 | tf_op jit(solution)/shard_map/pallas_call | solution.py:230
  216.7 2.8 collective-permute-done.12.own.refs_5_
  220.0 2.0 collective-permute-done.14.sib.refs_6_
  222.9 7.8 %shard_map.94.pre.refs_8_ = bf16[256,3072]{1,0:T(8,128)(2,1)} custom-call(s32[2]{0:T(128)} %pad_add_fusion.info, bf16[128,3072]{1,0:T(8,128)(2,1)} %collective-permute-done.12.own.refs_5_, bf16[128,3072]{1,0:T(8,128)(2,1)} %copy-done.12, bf16[3072,3072]{1,0:T(8,128)(2,1)} %w.22, bf16[256,1536]{1,0:T(8,128)(2,1)} %get-tuple-element.93.slope), custom_call_target="tpu_custom_call" | custom-call | flops 1 | bytes 1 | tf_op jit(solution)/shard_map/pallas_call | solution.py:202
  230.7 7.8 %shard_map.95 = (bf16[128,3072]{1,0:T(8,128)(2,1)}, bf16[128,3072]{1,0:T(8,128)(2,1)}) custom-call(s32[2]{0:T(128)} %pad_add_fusion.info, bf16[256,3072]{1,0:T(8,128)(2,1)} %shard_map.94.pre.refs_8_, bf16[3072,3072]{1,0:T(8,128)(2,1)} %w.23), custom_call_target="tpu_custom_call" | custom-call | flops 1 | bytes 1 | tf_op jit(solution)/shard_map/pallas_call | solution.py:230
  238.5 3.1 collective-permute-done.13.own.refs_10_
  242.6 1.6 collective-permute-done.17.sib.refs_11_
  244.2 7.7 %shard_map.96.pre.refs_13_ = bf16[256,3072]{1,0:T(8,128)(2,1)} custom-call(s32[2]{0:T(128)} %pad_add_fusion.info, bf16[128,3072]{1,0:T(8,128)(2,1)} %collective-permute-done.13.own.refs_10_, bf16[128,3072]{1,0:T(8,128)(2,1)} %collective-permute-done.17.sib.refs_11_, bf16[3072,3072]{1,0:T(8,128)(2,1)} %w.22, bf16[256,1536]{1,0:T(8,128)(2,1)} %get-tuple-element.99.slope), custom_call_target="tpu_custom_call" | custom-call | flops 1 | bytes 1 | tf_op jit(solution)/shard_map/pallas_call | solution.py:202
  251.9 7.7 %shard_map.97 = (bf16[128,3072]{1,0:T(8,128)(2,1)}, bf16[128,3072]{1,0:T(8,128)(2,1)}) custom-call(s32[2]{0:T(128)} %pad_add_fusion.info, bf16[256,3072]{1,0:T(8,128)(2,1)} %shard_map.96.pre.refs_13_, bf16[3072,3072]{1,0:T(8,128)(2,1)} %w.23), custom_call_target="tpu_custom_call" | custom-call | flops 1 | bytes 1 | tf_op jit(solution)/shard_map/pallas_call | solution.py:230
  259.6 3.9 collective-permute-done.16.own.refs_15_
  263.5 2.7 add_convert_fusion.7
  267.4 3.1 shard_map.98
  270.5 7.6 %shard_map.99.pre.refs_18_ = bf16[256,1536]{1,0:T(8,128)(2,1)} custom-call(s32[2]{0:T(128)} %pad_add_fusion.info, bf16[128,3072]{1,0:T(8,128)(2,1)} %copy-done.7, bf16[128,3072]{1,0:T(8,128)(2,1)} %copy-done.8, bf16[3072,3072]{1,0:T(8,128)(2,1)} %w.22, bf16[256,1536]{1,0:T(8,128)(2,1)} %get-tuple-element.107.slope), custom_call_target="tpu_custom_call" | custom-call | flops 1 | bytes 1 | tf_op jit(solution)/shard_map/pallas_call | solution.py:202
  278.1 9.9 %collective-permute-done.24 = bf16[128,3072]{1,0:T(8,128)(2,1)S(1)} collective-permute-done((bf16[128,3072]{1,0:T(8,128)(2,1)}, bf16[128,3072]{1,0:T(8,128)(2,1)S(1)}, u32[]{:S(2)}, u32[]{:S(2)}) %collective-permute-start.24) | collective-permute-done | bytes 786464 | tf_op jit(solution)/shard_map/ppermute | solution.py:325
  288.0 2.4 add_convert_fusion.6
  290.4 7.8 %shard_map.100 = (bf16[128,3072]{1,0:T(8,128)(2,1)}, bf16[128,3072]{1,0:T(8,128)(2,1)}) custom-call(s32[2]{0:T(128)} %pad_add_fusion.info, bf16[256,1536]{1,0:T(8,128)(2,1)} %shard_map.99.pre.refs_18_, bf16[3072,3072]{1,0:T(8,128)(2,1)} %w.23), custom_call_target="tpu_custom_call" | custom-call | flops 1 | bytes 1 | tf_op jit(solution)/shard_map/pallas_call | solution.py:230
  300.3 11.0 %collective-permute-done.25 = bf16[128,3072]{1,0:T(8,128)(2,1)} collective-permute-done((bf16[128,3072]{1,0:T(8,128)(2,1)}, bf16[128,3072]{1,0:T(8,128)(2,1)}, u32[]{:S(2)}, u32[]{:S(2)}) %collective-permute-start.25) | collective-permute-done | bytes 786464 | tf_op jit(solution)/shard_map/ppermute | solution.py:325
  311.8 2.6 add_convert_fusion.5
  315.1 3.6 collective-permute-done.27.refs_14_.refs_12_
  318.7 17.0 %collective-permute-done.32.refs_17_ = bf16[256,1536]{1,0:T(8,128)(2,1)} collective-permute-done((bf16[256,1536]{1,0:T(8,128)(2,1)}, bf16[256,1536]{1,0:T(8,128)(2,1)}, u32[]{:S(2)}, u32[]{:S(2)}) %collective-permute-start.32) | collective-permute-done | bytes 786464 | tf_op jit(solution)/shard_map/ppermute | solution.py:331
  335.6 12.5 %shard_map.104 = (bf16[384,1536]{1,0:T(8,128)(2,1)}, bf16[384,1536]{1,0:T(8,128)(2,1)}) custom-call(s32[3]{0:T(128)} %get-tuple-element.124.at, bf16[128,3072]{1,0:T(8,128)(2,1)} %bitcast.18, bf16[128,3072]{1,0:T(8,128)(2,1)} %collective-permute-done.3.sib.refs_1_, bf16[256,3072]{1,0:T(8,128)(2,1)} %collective-permute-done.15.refs_4_.refs_2_, ...), custom_call_target="tpu_custom_call" | custom-call | flops 1 | bytes 1 | tf_op jit(solution)/shard_map/pallas_call | solution.py:282
  349.0 12.5 %shard_map.103 = (bf16[384,1536]{1,0:T(8,128)(2,1)}, bf16[384,1536]{1,0:T(8,128)(2,1)}) custom-call(s32[3]{0:T(128)} %get-tuple-element.123.at, bf16[128,3072]{1,0:T(8,128)(2,1)} %bitcast.19, bf16[128,3072]{1,0:T(8,128)(2,1)} %collective-permute-done.3.sib.refs_1_, bf16[256,3072]{1,0:T(8,128)(2,1)} %collective-permute-done.15.refs_4_.refs_2_, ...), custom_call_target="tpu_custom_call" | custom-call | flops 1 | bytes 1 | tf_op jit(solution)/shard_map/pallas_call | solution.py:282
  362.3 12.5 %shard_map.101 = (bf16[384,1536]{1,0:T(8,128)(2,1)}, bf16[384,1536]{1,0:T(8,128)(2,1)}) custom-call(s32[3]{0:T(128)} %get-tuple-element.123.at, bf16[128,3072]{1,0:T(8,128)(2,1)} %bitcast.13, bf16[128,3072]{1,0:T(8,128)(2,1)} %copy-done.9, bf16[256,3072]{1,0:T(8,128)(2,1)} %copy-done.2, bf16[256,3072]{1,0:T(8,128)(2,1)} %shard_map.91.pre.refs_3_, ...), custom_call_target="tpu_custom_call" | custom-call | flops 1 | bytes 1 | tf_op jit(solution)/shard_map/pallas_call | solution.py:282
  374.9 12.5 %shard_map.102 = (bf16[384,1536]{1,0:T(8,128)(2,1)}, bf16[384,1536]{1,0:T(8,128)(2,1)}) custom-call(s32[3]{0:T(128)} %get-tuple-element.124.at, bf16[128,3072]{1,0:T(8,128)(2,1)} %bitcast.14, bf16[128,3072]{1,0:T(8,128)(2,1)} %copy-done.9, bf16[256,3072]{1,0:T(8,128)(2,1)} %copy-done.2, bf16[256,3072]{1,0:T(8,128)(2,1)} %shard_map.91.pre.refs_3_, ...), custom_call_target="tpu_custom_call" | custom-call | flops 1 | bytes 1 | tf_op jit(solution)/shard_map/pallas_call | solution.py:282
  387.5 1.2 collective-permute-start.29
  388.7 3.0 add_convert_fusion.4
  391.7 1.2 collective-permute-start.31
  393.6 1.7 maximum_select_fusion.1
  395.3 8.7 %collective-permute-done.29 = bf16[384,1536]{1,0:T(8,128)(2,1)S(1)} collective-permute-done((bf16[384,1536]{1,0:T(8,128)(2,1)}, bf16[384,1536]{1,0:T(8,128)(2,1)S(1)}, u32[]{:S(2)}, u32[]{:S(2)}) %collective-permute-start.29) | collective-permute-done | bytes 1179680 | tf_op jit(solution)/shard_map/ppermute | solution.py:424
  404.2 11.8 %collective-permute-done.31 = bf16[384,1536]{1,0:T(8,128)(2,1)S(1)} collective-permute-done((bf16[384,1536]{1,0:T(8,128)(2,1)S(1)}, bf16[384,1536]{1,0:T(8,128)(2,1)S(1)}, u32[]{:S(2)}, u32[]{:S(2)}) %collective-permute-start.31) | collective-permute-done | bytes 1179680 | tf_op jit(solution)/shard_map/ppermute | solution.py:425
  416.3 1.7 maximum_select_fusion
  (93 shorter events, 16.9 us)
Async XLA Ops:
  128.9 6.3 %collective-permute-start.1 = (bf16[128,3072]{1,0:T(8,128)(2,1)}, bf16[128,3072]{1,0:T(8,128)(2,1)S(1)}, u32[]{:S(2)}, u32[]{:S(2)}) collective-permute-start(bf16[128,3072]{1,0:T(8,128)(2,1)} %bitcast.10), channel_id=1, source_target_pairs={{0,4},{4,0},{8,12},{12,8},{16,20},{20,16},{24,28},{28,24},{1,5},{5... | collective-permute-start | bytes 2359304 | tf_op jit(solution)/shard_map/ppermute | solution.py:328
  128.9 22.6 %collective-permute-start = (bf16[128,3072]{1,0:T(8,128)(2,1)}, bf16[128,3072]{1,0:T(8,128)(2,1)}, u32[]{:S(2)}, u32[]{:S(2)}) collective-permute-start(bf16[128,3072]{1,0:T(8,128)(2,1)} %bitcast.11), channel_id=1, source_target_pairs={{0,1},{1,2},{2,3},{3,0},{4,5},{5,6},{6,7},{7,4},{8,9},{9,10},{10,1... | collective-permute-start | bytes 2359304 | tf_op jit(solution)/shard_map/ppermute | solution.py:325
  130.9 32.6 %all-to-all-start.1 = ((bf16[8,32,3072]{2,1,0:T(8,128)(2,1)}), bf16[8,32,3072]{2,1,0:T(8,128)(2,1)}, u32[]{:S(2)}, u32[]{:S(2)}) async-start(bf16[8,32,3072]{2,1,0:T(8,128)(2,1)} %get-tuple-element.65), calls=%async_computation.1 | async-start | bytes 3145728 | tf_op jit(solution)/shard_map/all_to_all | solution.py:322
  151.5 2.5 collective-permute-start.2
  151.5 22.1 %collective-permute-start.4 = (bf16[128,3072]{1,0:T(8,128)(2,1)}, bf16[128,3072]{1,0:T(8,128)(2,1)}, u32[]{:S(2)}, u32[]{:S(2)}) collective-permute-start(bf16[128,3072]{1,0:T(8,128)(2,1)} %collective-permute-done.own.refs_5_), channel_id=1, source_target_pairs={{0,1},{1,2},{2,3},{3,0},{4,5},{5,6},{6,7},{7,4},{8,9},{9,10},{10,1... | collective-permute-start | bytes 2359304 | tf_op jit(solution)/shard_map/ppermute | solution.py:325
  151.5 22.6 %collective-permute-start.6 = (bf16[256,3072]{1,0:T(8,128)(2,1)}, bf16[256,3072]{1,0:T(8,128)(2,1)S(1)}, u32[]{:S(2)}, u32[]{:S(2)}) collective-permute-start(bf16[256,3072]{1,0:T(8,128)(2,1)} %get-tuple-element.69.refs_3_), channel_id=1, source_target_pairs={{0,8},{4,20},{8,0},{12,28},{16,24},{20,4},{24,16},{28,12},{1,9},{5... | collective-permute-start | bytes 4718600 | tf_op jit(solution)/shard_map/ppermute | solution.py:331
  163.0 26.0 %collective-permute-start.7 = (bf16[256,3072]{1,0:T(8,128)(2,1)}, bf16[256,3072]{1,0:T(8,128)(2,1)S(1)}, u32[]{:S(2)}, u32[]{:S(2)}) collective-permute-start(bf16[256,3072]{1,0:T(8,128)(2,1)} %get-tuple-element.73.refs_8_), channel_id=1, source_target_pairs={{0,8},{4,20},{8,0},{12,28},{16,24},{20,4},{24,16},{28,12},{1,9},{5... | collective-permute-start | bytes 4718600 | tf_op jit(solution)/shard_map/ppermute | solution.py:331
  173.6 2.6 collective-permute-start.5
  173.6 11.2 %collective-permute-start.3 = (bf16[128,3072]{1,0:T(8,128)(2,1)}, bf16[128,3072]{1,0:T(8,128)(2,1)}, u32[]{:S(2)}, u32[]{:S(2)}) collective-permute-start(bf16[128,3072]{1,0:T(8,128)(2,1)} %bitcast.15), channel_id=1, source_target_pairs={{0,4},{4,0},{8,12},{12,8},{16,20},{20,16},{24,28},{28,24},{1,5},{5... | collective-permute-start | bytes 2359304 | tf_op jit(solution)/shard_map/ppermute | solution.py:328
  174.1 22.6 %collective-permute-start.8 = (bf16[128,3072]{1,0:T(8,128)(2,1)}, bf16[128,3072]{1,0:T(8,128)(2,1)}, u32[]{:S(2)}, u32[]{:S(2)}) collective-permute-start(bf16[128,3072]{1,0:T(8,128)(2,1)} %collective-permute-done.4.own.refs_10_), channel_id=1, source_target_pairs={{0,1},{1,2},{2,3},{3,0},{4,5},{5,6},{6,7},{7,4},{8,9},{9,10},{10,1... | collective-permute-start | bytes 2359304 | tf_op jit(solution)/shard_map/ppermute | solution.py:325
  174.1 10.2 %copy-start.2 = (bf16[256,3072]{1,0:T(8,128)(2,1)}, bf16[256,3072]{1,0:T(8,128)(2,1)S(1)}, u32[]{:S(2)}) copy-start(bf16[256,3072]{1,0:T(8,128)(2,1)S(1)} %collective-permute-done.6.refs_2_.refs_4_) | copy-start | bytes 4718596
  184.2 24.7 %collective-permute-start.10 = (bf16[256,3072]{1,0:T(8,128)(2,1)}, bf16[256,3072]{1,0:T(8,128)(2,1)S(1)}, u32[]{:S(2)}, u32[]{:S(2)}) collective-permute-start(bf16[256,3072]{1,0:T(8,128)(2,1)} %get-tuple-element.78.refs_13_), channel_id=1, source_target_pairs={{0,8},{4,20},{8,0},{12,28},{16,24},{20,4},{24,16},{28,12},{1,9},{5... | collective-permute-start | bytes 4718600 | tf_op jit(solution)/shard_map/ppermute | solution.py:331
  189.0 7.7 %copy-start.3 = (bf16[256,3072]{1,0:T(8,128)(2,1)}, bf16[256,3072]{1,0:T(8,128)(2,1)S(1)}, u32[]{:S(2)}) copy-start(bf16[256,3072]{1,0:T(8,128)(2,1)S(1)} %collective-permute-done.7.refs_7_.refs_9_) | copy-start | bytes 4718596
  196.7 3.3 collective-permute-start.9
  197.9 21.6 %collective-permute-start.12 = (bf16[128,3072]{1,0:T(8,128)(2,1)}, bf16[128,3072]{1,0:T(8,128)(2,1)}, u32[]{:S(2)}, u32[]{:S(2)}) collective-permute-start(bf16[128,3072]{1,0:T(8,128)(2,1)} %bitcast.17), channel_id=1, source_target_pairs={{0,1},{1,2},{2,3},{3,0},{4,5},{5,6},{6,7},{7,4},{8,9},{9,10},{10,1... | collective-permute-start | bytes 2359304 | tf_op jit(solution)/shard_map/ppermute | solution.py:325
  199.5 31.2 %collective-permute-start.15 = (bf16[256,3072]{1,0:T(8,128)(2,1)}, bf16[256,3072]{1,0:T(8,128)(2,1)}, u32[]{:S(2)}, u32[]{:S(2)}) collective-permute-start(bf16[256,3072]{1,0:T(8,128)(2,1)} %shard_map.91.pre.refs_3_), channel_id=1, source_target_pairs={{0,8},{4,20},{8,0},{12,28},{16,24},{20,4},{24,16},{28,12},{1,9},{5... | collective-permute-start | bytes 4718600 | tf_op jit(solution)/shard_map/ppermute | solution.py:331
  209.0 7.7 %copy-start.4 = (bf16[256,3072]{1,0:T(8,128)(2,1)}, bf16[256,3072]{1,0:T(8,128)(2,1)S(1)}, u32[]{:S(2)}) copy-start(bf16[256,3072]{1,0:T(8,128)(2,1)S(1)} %collective-permute-done.10.refs_12_.refs_14_) | copy-start | bytes 4718596
  219.5 2.5 collective-permute-start.14
  219.5 22.1 %collective-permute-start.13 = (bf16[128,3072]{1,0:T(8,128)(2,1)}, bf16[128,3072]{1,0:T(8,128)(2,1)}, u32[]{:S(2)}, u32[]{:S(2)}) collective-permute-start(bf16[128,3072]{1,0:T(8,128)(2,1)} %collective-permute-done.12.own.refs_5_), channel_id=1, source_target_pairs={{0,1},{1,2},{2,3},{3,0},{4,5},{5,6},{6,7},{7,4},{8,9},{9,10},{10,1... | collective-permute-start | bytes 2359304 | tf_op jit(solution)/shard_map/ppermute | solution.py:325
  219.5 32.4 %collective-permute-start.18 = (bf16[256,3072]{1,0:T(8,128)(2,1)}, bf16[256,3072]{1,0:T(8,128)(2,1)S(1)}, u32[]{:S(2)}, u32[]{:S(2)}) collective-permute-start(bf16[256,3072]{1,0:T(8,128)(2,1)} %get-tuple-element.85.refs_18_), channel_id=1, source_target_pairs={{0,8},{4,20},{8,0},{12,28},{16,24},{20,4},{24,16},{28,12},{1,9},{5... | collective-permute-start | bytes 4718600 | tf_op jit(solution)/shard_map/ppermute | solution.py:331
  230.6 11.4 %copy-start = (bf16[256,3072]{1,0:T(8,128)(2,1)S(1)}, bf16[256,3072]{1,0:T(8,128)(2,1)}, u32[]{:S(2)}) copy-start(bf16[256,3072]{1,0:T(8,128)(2,1)} %shard_map.94.pre.refs_8_) | copy-start | bytes 4718596
  241.6 2.6 collective-permute-start.17
  241.6 18.1 %collective-permute-start.23 = (bf16[128,3072]{1,0:T(8,128)(2,1)}, bf16[128,3072]{1,0:T(8,128)(2,1)}, u32[]{:S(2)}, u32[]{:S(2)}) collective-permute-start(bf16[128,3072]{1,0:T(8,128)(2,1)} %get-tuple-element.95), channel_id=1, source_target_pairs={{0,4},{4,0},{8,12},{12,8},{16,20},{20,16},{24,28},{28,24},{1,5},{5... | collective-permute-start | bytes 2359304 | tf_op jit(solution)/shard_map/ppermute | solution.py:328
  242.1 21.5 %collective-permute-start.16 = (bf16[128,3072]{1,0:T(8,128)(2,1)}, bf16[128,3072]{1,0:T(8,128)(2,1)S(1)}, u32[]{:S(2)}, u32[]{:S(2)}) collective-permute-start(bf16[128,3072]{1,0:T(8,128)(2,1)} %collective-permute-done.13.own.refs_10_), channel_id=1, source_target_pairs={{0,1},{1,2},{2,3},{3,0},{4,5},{5,6},{6,7},{7,4},{8,9},{9,10},{10,1... | collective-permute-start | bytes 2359304 | tf_op jit(solution)/shard_map/ppermute | solution.py:325
  242.1 28.4 %collective-permute-start.20 = (bf16[256,3072]{1,0:T(8,128)(2,1)S(1)}, bf16[256,3072]{1,0:T(8,128)(2,1)}, u32[]{:S(2)}, u32[]{:S(2)}) collective-permute-start(bf16[256,3072]{1,0:T(8,128)(2,1)S(1)} %copy-done), channel_id=1, source_target_pairs={{0,8},{4,20},{8,0},{12,28},{16,24},{20,4},{24,16},{28,12},{1,9},{5... | collective-permute-start | bytes 4718600 | tf_op jit(solution)/shard_map/ppermute | solution.py:331
  251.9 7.7 %copy-start.5 = (bf16[256,3072]{1,0:T(8,128)(2,1)}, bf16[256,3072]{1,0:T(8,128)(2,1)S(1)}, u32[]{:S(2)}) copy-start(bf16[256,3072]{1,0:T(8,128)(2,1)S(1)} %collective-permute-done.18.refs_17_.refs_19_) | copy-start | bytes 4718596
  263.5 3.0 collective-permute-start.19
  266.3 21.7 %collective-permute-start.24 = (bf16[128,3072]{1,0:T(8,128)(2,1)}, bf16[128,3072]{1,0:T(8,128)(2,1)S(1)}, u32[]{:S(2)}, u32[]{:S(2)}) collective-permute-start(bf16[128,3072]{1,0:T(8,128)(2,1)} %add_convert_fusion.7), channel_id=1, source_target_pairs={{0,1},{1,2},{2,3},{3,0},{4,5},{5,6},{6,7},{7,4},{8,9},{9,10},{10,1... | collective-permute-start | bytes 2359304 | tf_op jit(solution)/shard_map/ppermute | solution.py:325
  266.3 21.7 %collective-permute-start.22 = (bf16[128,3072]{1,0:T(8,128)(2,1)}, bf16[128,3072]{1,0:T(8,128)(2,1)}, u32[]{:S(2)}, u32[]{:S(2)}) collective-permute-start(bf16[128,3072]{1,0:T(8,128)(2,1)} %get-tuple-element.101), channel_id=1, source_target_pairs={{0,4},{4,0},{8,12},{12,8},{16,20},{20,16},{24,28},{28,24},{1,5},{5... | collective-permute-start | bytes 2359304 | tf_op jit(solution)/shard_map/ppermute | solution.py:328
  270.5 17.5 %copy-start.15 = (bf16[128,3072]{1,0:T(8,128)(2,1)S(1)}, bf16[128,3072]{1,0:T(8,128)(2,1)}, u32[]{:S(2)}) copy-start(bf16[128,3072]{1,0:T(8,128)(2,1)} %get-tuple-element.111) | copy-start | bytes 2359300
  290.4 7.8 %copy-start.1 = (bf16[256,3072]{1,0:T(8,128)(2,1)S(1)}, bf16[256,3072]{1,0:T(8,128)(2,1)}, u32[]{:S(2)}) copy-start(bf16[256,3072]{1,0:T(8,128)(2,1)} %shard_map.96.pre.refs_13_) | copy-start | bytes 4718596
  290.4 21.0 %collective-permute-start.25 = (bf16[128,3072]{1,0:T(8,128)(2,1)}, bf16[128,3072]{1,0:T(8,128)(2,1)}, u32[]{:S(2)}, u32[]{:S(2)}) collective-permute-start(bf16[128,3072]{1,0:T(8,128)(2,1)} %add_convert_fusion.6), channel_id=1, source_target_pairs={{0,1},{1,2},{2,3},{3,0},{4,5},{5,6},{6,7},{7,4},{8,9},{9,10},{10,1... | collective-permute-start | bytes 2359304 | tf_op jit(solution)/shard_map/ppermute | solution.py:325
  298.2 13.6 %collective-permute-start.21 = (bf16[128,3072]{1,0:T(8,128)(2,1)}, bf16[128,3072]{1,0:T(8,128)(2,1)S(1)}, u32[]{:S(2)}, u32[]{:S(2)}) collective-permute-start(bf16[128,3072]{1,0:T(8,128)(2,1)} %get-tuple-element.110), channel_id=1, source_target_pairs={{0,4},{4,0},{8,12},{12,8},{16,20},{20,16},{24,28},{28,24},{1,5},{5... | collective-permute-start | bytes 2359304 | tf_op jit(solution)/shard_map/ppermute | solution.py:328
  298.2 20.5 %collective-permute-start.27 = (bf16[256,3072]{1,0:T(8,128)(2,1)S(1)}, bf16[256,3072]{1,0:T(8,128)(2,1)S(1)}, u32[]{:S(2)}, u32[]{:S(2)}) collective-permute-start(bf16[256,3072]{1,0:T(8,128)(2,1)S(1)} %copy-done.1), channel_id=1, source_target_pairs={{0,8},{4,20},{8,0},{12,28},{16,24},{20,4},{24,16},{28,12},{1,9},{5... | collective-permute-start | bytes 4718600 | tf_op jit(solution)/shard_map/ppermute | solution.py:331
  298.8 88.6 %collective-permute-start.11 = (bf16[128,3072]{1,0:T(8,128)(2,1)}, bf16[128,3072]{1,0:T(8,128)(2,1)}, u32[]{:S(2)}, u32[]{:S(2)}) collective-permute-start(bf16[128,3072]{1,0:T(8,128)(2,1)} %get-tuple-element.88), channel_id=1, source_target_pairs={{0,4},{4,0},{8,12},{12,8},{16,20},{20,16},{24,28},{28,24},{1,5},{5... | collective-permute-start | bytes 2359304 | tf_op jit(solution)/shard_map/ppermute | solution.py:328
  299.2 62.3 %collective-permute-start.28 = (bf16[256,1536]{1,0:T(8,128)(2,1)}, bf16[256,1536]{1,0:T(8,128)(2,1)}, u32[]{:S(2)}, u32[]{:S(2)}) collective-permute-start(bf16[256,1536]{1,0:T(8,128)(2,1)} %shard_map.99.pre.refs_18_), channel_id=1, source_target_pairs={{0,8},{4,20},{8,0},{12,28},{16,24},{20,4},{24,16},{28,12},{1,9},{5... | collective-permute-start | bytes 2359304 | tf_op jit(solution)/shard_map/ppermute | solution.py:331
  311.3 24.3 %collective-permute-start.32 = (bf16[256,1536]{1,0:T(8,128)(2,1)}, bf16[256,1536]{1,0:T(8,128)(2,1)}, u32[]{:S(2)}, u32[]{:S(2)}) collective-permute-start(bf16[256,1536]{1,0:T(8,128)(2,1)} %shard_map.98), channel_id=1, source_target_pairs={{0,8},{4,20},{8,0},{12,28},{16,24},{20,4},{24,16},{28,12},{1,9},{5... | collective-permute-start | bytes 2359304 | tf_op jit(solution)/shard_map/ppermute | solution.py:331
  314.4 73.0 %collective-permute-start.26 = (bf16[128,3072]{1,0:T(8,128)(2,1)}, bf16[128,3072]{1,0:T(8,128)(2,1)}, u32[]{:S(2)}, u32[]{:S(2)}) collective-permute-start(bf16[128,3072]{1,0:T(8,128)(2,1)} %add_convert_fusion.5), channel_id=1, source_target_pairs={{0,1},{1,2},{2,3},{3,0},{4,5},{5,6},{6,7},{7,4},{8,9},{9,10},{10,1... | collective-permute-start | bytes 2359304 | tf_op jit(solution)/shard_map/ppermute | solution.py:325
  318.7 17.0 %copy-start.6 = (bf16[256,3072]{1,0:T(8,128)(2,1)}, bf16[256,3072]{1,0:T(8,128)(2,1)S(1)}, u32[]{:S(2)}) copy-start(bf16[256,3072]{1,0:T(8,128)(2,1)S(1)} %collective-permute-done.27.refs_14_.refs_12_) | copy-start | bytes 4718596
  348.2 43.5 %collective-permute-start.33 = (bf16[384,1536]{1,0:T(8,128)(2,1)}, bf16[384,1536]{1,0:T(8,128)(2,1)S(1)}, u32[]{:S(2)}, u32[]{:S(2)}) collective-permute-start(bf16[384,1536]{1,0:T(8,128)(2,1)} %get-tuple-element.120), channel_id=1, source_target_pairs={{0,16},{4,12},{8,24},{12,4},{16,0},{20,28},{24,8},{28,20},{1,17},{... | collective-permute-start | bytes 3538952 | tf_op jit(solution)/shard_map/ppermute | solution.py:424
  349.0 44.2 %collective-permute-start.35 = (bf16[384,1536]{1,0:T(8,128)(2,1)}, bf16[384,1536]{1,0:T(8,128)(2,1)S(1)}, u32[]{:S(2)}, u32[]{:S(2)}) collective-permute-start(bf16[384,1536]{1,0:T(8,128)(2,1)} %get-tuple-element.122), channel_id=1, source_target_pairs={{0,20},{4,8},{8,28},{12,0},{16,4},{20,24},{24,12},{28,16},{1,21},{... | collective-permute-start | bytes 3538952 | tf_op jit(solution)/shard_map/ppermute | solution.py:425
  361.6 31.7 %collective-permute-start.34 = (bf16[384,1536]{1,0:T(8,128)(2,1)}, bf16[384,1536]{1,0:T(8,128)(2,1)S(1)}, u32[]{:S(2)}, u32[]{:S(2)}) collective-permute-start(bf16[384,1536]{1,0:T(8,128)(2,1)} %get-tuple-element.121), channel_id=1, source_target_pairs={{0,4},{4,0},{8,12},{12,8},{16,20},{20,16},{24,28},{28,24},{1,5},{5... | collective-permute-start | bytes 3538952 | tf_op jit(solution)/shard_map/ppermute | solution.py:328
  387.4 16.9 %collective-permute-start.30 = (bf16[384,1536]{1,0:T(8,128)(2,1)}, bf16[384,1536]{1,0:T(8,128)(2,1)S(1)}, u32[]{:S(2)}, u32[]{:S(2)}) collective-permute-start(bf16[384,1536]{1,0:T(8,128)(2,1)} %get-tuple-element.117), channel_id=1, source_target_pairs={{0,4},{4,0},{8,12},{12,8},{16,20},{20,16},{24,28},{28,24},{1,5},{5... | collective-permute-start | bytes 3538952 | tf_op jit(solution)/shard_map/ppermute | solution.py:328
  387.5 16.5 %collective-permute-start.29 = (bf16[384,1536]{1,0:T(8,128)(2,1)}, bf16[384,1536]{1,0:T(8,128)(2,1)S(1)}, u32[]{:S(2)}, u32[]{:S(2)}) collective-permute-start(bf16[384,1536]{1,0:T(8,128)(2,1)} %get-tuple-element.116), channel_id=1, source_target_pairs={{0,16},{4,12},{8,24},{12,4},{16,0},{20,28},{24,8},{28,20},{1,17},{... | collective-permute-start | bytes 3538952 | tf_op jit(solution)/shard_map/ppermute | solution.py:424
  388.7 3.0 copy-start.16
  388.7 4.2 %copy-start.13 = (bf16[384,1536]{1,0:T(8,128)(2,1)S(1)}, bf16[384,1536]{1,0:T(8,128)(2,1)}, u32[]{:S(2)}) copy-start(bf16[384,1536]{1,0:T(8,128)(2,1)} %get-tuple-element.119) | copy-start | bytes 3538948
  391.7 24.3 %collective-permute-start.31 = (bf16[384,1536]{1,0:T(8,128)(2,1)S(1)}, bf16[384,1536]{1,0:T(8,128)(2,1)S(1)}, u32[]{:S(2)}, u32[]{:S(2)}) collective-permute-start(bf16[384,1536]{1,0:T(8,128)(2,1)S(1)} %copy-done.16), channel_id=1, source_target_pairs={{0,20},{4,8},{8,28},{12,0},{16,4},{20,24},{24,12},{28,16},{1,21},{... | collective-permute-start | bytes 3538952 | tf_op jit(solution)/shard_map/ppermute | solution.py:425
  393.5 10.4 %copy-start.14 = (bf16[384,1536]{1,0:T(8,128)(2,1)S(1)}, bf16[384,1536]{1,0:T(8,128)(2,1)}, u32[]{:S(2)}) copy-start(bf16[384,1536]{1,0:T(8,128)(2,1)} %get-tuple-element.115) | copy-start | bytes 3538948
  (6 other events, 7.4 us)

commit v2 on v1

--- a/solution.py
+++ b/solution.py
@@ -45,36 +45,34 @@
     return source
 
 
-def pack_body(info, count, x, g, x_out, g_out, sems):
-    dp, blocks = x_out.shape[0], x.shape[0]
+def pack_body(info, count, rows, out, sems):
+    dp, blocks = out.shape[0], rows.shape[0]
     start = start_of(count, info[0], dp)
     copies = []
-    for t, (rows, out) in enumerate(((x, x_out), (g, g_out))):
-        for k in range(dp):
-            block = jnp.minimum(lax.rem(k + OWNB * dp - start, dp), blocks - 1)
-            copies.append(pltpu.make_async_copy(rows.at[block], out.at[k], sems.at[t, k]))
+    for k in range(dp):
+        block = jnp.minimum(lax.rem(k + OWNB * dp - start, dp), blocks - 1)
+        copies.append(pltpu.make_async_copy(rows.at[block], out.at[k], sems.at[k]))
     for copy in copies:
         copy.start()
     for copy in copies:
         copy.wait()
 
 
-def pack(x_rows, g_rows, info, count, dp):
-    _, here, d = x_rows.shape
-    shape = jax.ShapeDtypeStruct((dp, here, d), BF16)
-    any_spec = pl.BlockSpec(memory_space=pl.ANY)
+def pack(rows, info, count, dp):
+    _, here, d = rows.shape
     return pl.pallas_call(
         pack_body,
-        out_shape=(shape, shape),
+        out_shape=jax.ShapeDtypeStruct((dp, here, d), BF16),
         grid_spec=pltpu.PrefetchScalarGridSpec(
             num_scalar_prefetch=2,
-            in_specs=[any_spec, any_spec],
-            out_specs=(any_spec, any_spec),
-            scratch_shapes=[pltpu.SemaphoreType.DMA((2, dp))],
-        ),
-        compiler_params=pltpu.CompilerParams(vmem_limit_bytes=VMEM_LIMIT),
-        cost_estimate=SHORT,
-    )(info, count, x_rows, g_rows)
+            grid=(1,),
+            in_specs=[pl.BlockSpec(memory_space=pl.ANY)],
+            out_specs=pl.BlockSpec((dp, here, d), lambda n, i, c: (0, 0, 0)),
+            scratch_shapes=[pltpu.SemaphoreType.DMA((dp,))],
+        ),
+        compiler_params=pltpu.CompilerParams(vmem_limit_bytes=VMEM_LIMIT),
+        cost_estimate=SHORT,
+    )(info, count, rows)
 
 
 def select_body(info, count, patches, rows, out, *, dp):
@@ -124,7 +122,7 @@
         out[:, hidden + j * width:hidden + (j + 1) * width] = rows[:, pl.ds(at, width)]
 
 
-def up_body(info, own, sib, w, out, slope, rows, *, hidden, chips):
+def up_body(info, own, sib, w, out, rows, slope, *, hidden, chips):
     n = pl.program_id(0)
 
     @pl.when(n == 0)
@@ -183,8 +181,11 @@
     width = block_of(hidden, 768)
     steps = hidden // width
     across = hidden + (d // 2 if with_columns else 0)
-    out_shape = jax.ShapeDtypeStruct((2 * half, across), BF16)
-    out_spec = pl.BlockSpec((2 * half, across), lambda n, i: (0, 0))
+    out_shape = (jax.ShapeDtypeStruct((2 * half, across), BF16), jax.ShapeDtypeStruct((2 * half, d), BF16))
+    out_specs = (
+        pl.BlockSpec((2 * half, across), lambda n, i: (0, 0)),
+        pl.BlockSpec((2 * half, d), lambda n, i: (0, 0)),
+    )
     slope_spec = pl.BlockSpec((2 * half, width), lambda n, i: (0, n))
     rows_spec = pl.BlockSpec((half, d), lambda n, i: (0, 0))
     w_spec = pl.BlockSpec((d, width), lambda n, i: (0, (i[0] & 1) * steps + n))
@@ -192,11 +193,10 @@
     operands = [own, sib, w]
     if slope is None:
         body = up_body
-        out_shape = (out_shape, jax.ShapeDtypeStruct((2 * half, hidden), BF16))
-        out_specs = (out_spec, slope_spec)
+        out_shape += (jax.ShapeDtypeStruct((2 * half, hidden), BF16),)
+        out_specs += (slope_spec,)
     else:
         body = down_body
-        out_specs = out_spec
         in_specs.append(slope_spec)
         operands.append(slope)
     return pl.pallas_call(
@@ -207,7 +207,6 @@
             grid=(steps,),
             in_specs=in_specs,
             out_specs=out_specs,
-            scratch_shapes=[pltpu.VMEM((2 * half, d), BF16)],
         ),
         compiler_params=pltpu.CompilerParams(vmem_limit_bytes=VMEM_LIMIT),
         cost_estimate=SHORT,
@@ -244,49 +243,63 @@
     )(info, pre, w)
 
 
-def weight_body(at, *refs, slots):
-    ins, (straight, crossed) = refs[:5 * slots], refs[5 * slots:]
-    total = None
-    dims = (((0,), (0,)), ((), ()))
+def weight_body(at, *refs, begins, width, block):
+    slots = len(begins)
+    ins, (straight, crossed, left, right, left_sems, right_sems) = refs[:4 * slots], refs[4 * slots:]
+    steps, size = right.shape[0], ins[0].shape[0]
+    left_copies, right_copies = [], [[] for _ in range(steps)]
     for s in range(slots):
-        own, sib, there, mine, theirs = ins[5 * s:5 * s + 5]
-        half = own.shape[0]
-        for left, right in ((own[...], mine[:half]), (sib[...], mine[half:]), (there[...], theirs[...])):
-            term = lax.dot_general(left, right, dims, preferred_element_type=F32)
-            total = term if total is None else total + term
-    span = straight.shape[0]
-    low, high = total[:span], total[span:]
+        own, there, mine, theirs = ins[4 * s:4 * s + 4]
+        columns = (at[0] * width, begins[s] + at[1] * width)
+        for k, (rows, hidden_side) in enumerate(((own, mine), (there, theirs))):
+            to = pl.ds((2 * s + k) * size, size)
+            source = rows.at[:, pl.ds(pl.multiple_of(columns[k], 128), width)]
+            left_copies.append(pltpu.make_async_copy(source, left.at[to], left_sems.at[2 * s + k]))
+            for n in range(steps):
+                source = hidden_side.at[:, pl.ds(n * block, block)]
+                right_copies[n].append(
+                    pltpu.make_async_copy(source, right.at[n, to], right_sems.at[n, 2 * s + k])
+                )
+    for copies in (left_copies, *right_copies):
+        for copy in copies:
+            copy.start()
+    for copy in left_copies:
+        copy.wait()
+    span = width // 2
     first = at[2] == 0
-    straight[...] = jnp.where(first, low, high).astype(straight.dtype)
-    crossed[...] = jnp.where(first, high, low).astype(crossed.dtype)
+    for n in range(steps):
+        for copy in right_copies[n]:
+            copy.wait()
+        total = lax.dot_general(left[...], right[n], (((0,), (0,)), ((), ())), preferred_element_type=F32)
+        low, high = total[:span], total[span:]
+        straight[:, n * block:(n + 1) * block] = jnp.where(first, low, high).astype(straight.dtype)
+        crossed[:, n * block:(n + 1) * block] = jnp.where(first, high, low).astype(crossed.dtype)
 
 
 def weight_part(rows, there_rows, rights, own_at, there_at, core, width, hidden):
-    slots = len(rows)
+    slots, size = len(rows), rows[0].shape[0]
     at = jnp.stack([own_at, there_at, core]).astype(jnp.int32)
     block = block_of(hidden, 512)
-    operands, specs = [], []
-    for (own, sib), (there, begin), (mine, theirs) in zip(rows, there_rows, rights):
-        half = own.shape[0]
-        operands += [own, sib, there, mine, theirs]
-        specs += [
-            pl.BlockSpec((half, width), lambda n, a: (0, a[0])),
-            pl.BlockSpec((half, width), lambda n, a: (0, a[0])),
-            pl.BlockSpec((2 * half, width), lambda n, a, first=begin // width: (0, first + a[1])),
-            pl.BlockSpec((2 * half, block), lambda n, a: (0, n)),
-            pl.BlockSpec((2 * half, block), lambda n, a: (0, n)),
-        ]
-    total = 4 * half * slots
+    steps = hidden // block
+    operands = []
+    for own, (there, _), (mine, theirs) in zip(rows, there_rows, rights):
+        operands += [own, there, mine, theirs]
     shape = jax.ShapeDtypeStruct((width // 2, hidden), BF16)
-    spec = pl.BlockSpec((width // 2, block), lambda n, a: (0, n))
-    return pl.pallas_call(
-        functools.partial(weight_body, slots=slots),
+    spec = pl.BlockSpec((width // 2, hidden), lambda n, a: (0, 0))
+    return pl.pallas_call(
+        functools.partial(weight_body, begins=[begin for _, begin in there_rows], width=width, block=block),
         out_shape=(shape, shape),
         grid_spec=pltpu.PrefetchScalarGridSpec(
             num_scalar_prefetch=1,
-            grid=(hidden // block,),
-            in_specs=specs,
+            grid=(1,),
+            in_specs=[pl.BlockSpec(memory_space=pl.ANY)] * len(operands),
             out_specs=(spec, spec),
+            scratch_shapes=[
+                pltpu.VMEM((2 * slots * size, width), BF16),
+                pltpu.VMEM((steps, 2 * slots * size, block), BF16),
+                pltpu.SemaphoreType.DMA((2 * slots,)),
+                pltpu.SemaphoreType.DMA((steps, 2 * slots)),
+            ],
         ),
         compiler_params=pltpu.CompilerParams(vmem_limit_bytes=VMEM_LIMIT),
         cost_estimate=SHORT,
@@ -333,104 +346,132 @@
     def chosen(arrived):
         return done(select(after(arrived), info, block_count, patches)).reshape(OWNB * here, d)
 
-    send_x, send_g = pack(x_rows, g_rows, info, block_count, dp)
-    arrived_x = done(exchange(send_x))
-    arrived_g = exchange(after(send_g))
-    x_own = [chosen(arrived_x)]
-    x_sib, g_own, g_sib = [sibling(x_own[0])], [], []
-    x_ahead = onward(x_own[0])
-    act, slope, pre, shares = [], [], [], []
-
-    def up(s):
-        mine, slope_s = forward(*after(x_own[s], x_sib[s]), w_up, info, chips)
-        slope.append(slope_s)
-        act.append((mine, pooled(done(mine))))
-
-    def down(s, with_columns=True):
-        mine = done(forward(*after(g_own[s], g_sib[s]), w_down_t, info, chips, slope[s], with_columns))
-        pre.append((mine, pooled(mine)))
-
-    def share(s):
-        own, sib = input_part(after(pre[s][0]), w_up, info)
-        shares.append((own, sibling(done(sib))))
-
     def arrive(own, sib, ahead, further=True):
         piece = after(ahead)
         own.append(piece)
         sib.append(sibling(piece))
         return onward(piece) if further else None
 
-    def settle(pairs, s):
-        if 0 <= s < len(pairs):
-            last.append(pairs[s][1])
-
+    x_own, x_sib, x_rows_of, x_there = [], [], [], []
+    g_own, g_sib, g_rows_of, g_there = [], [], [], []
+    act, slope, pre, shares, pools = [], [], [], [], {}
+
+    def settle(*names):
+        last.extend(pools[name] for name in names if name in pools)
+
+    def up(s):
+        mine, rows, slope_s = forward(*after(x_own[s], x_sib[s]), w_up, info, chips)
+        theirs = pools["x", s] = pooled(done(mine))
+        x_rows_of.append(rows)
+        x_there.append((theirs, hidden))
+        slope.append(slope_s)
+        act.append((mine, theirs))
+
+    def down(s, with_columns=True):
+        mine, rows = forward(*after(g_own[s], g_sib[s]), w_down_t, info, chips, slope[s], with_columns)
+        theirs = pools["g", s] = pooled(done(mine))
+        g_rows_of.append(rows)
+        if with_columns:
+            g_there.append((theirs, hidden))
+        pre.append((mine, theirs))
+
+    def share(s):
+        own, sib = input_part(after(pre[s][0]), w_up, info)
+        pools["share", s] = sibling(done(sib))
+        shares.append((own, pools["share", s]))
+
+    send_x = done(pack(x_rows, info, block_count, dp))
+    arrived_x = exchange(send_x)
+    send_g = done(pack(after(g_rows), info, block_count, dp))
+    arrived_g = exchange(lax.optimization_barrier((send_g, arrived_x))[0])
+    x_own.append(chosen(arrived_x))
+    x_sib.append(sibling(x_own[0]))
+    x_ahead = onward(x_own[0])
     up(0)
+    end = tensor - 1
     for s in range(1, tensor):
-        x_ahead = arrive(x_own, x_sib, x_ahead, s + 1 < tensor)
-        if s == tensor - 1:
+        x_ahead = arrive(x_own, x_sib, x_ahead, s < end)
+        if s == end:
             g_ahead = onward(after(g_own[0]))
-        settle(act, s - 2)
+        settle(("x", s - 2))
         up(s)
         if s == 1:
             g_own.append(chosen(arrived_g))
             g_sib.append(sibling(g_own[0]))
         if s == 2:
-            settle(act, 1)
+            settle(("x", 1))
             down(0)
-    settle(act, tensor - 2)
+    settle(("x", end - 1))
     share(0)
-    g_last = None
-    for s in range(1, tensor):
-        g_ahead = arrive(g_own, g_sib, g_ahead, s + 1 < tensor)
-        if s == tensor - 1:
-            running = onward(add(*after(*shares[1])))
-            g_last = partner_columns(*after(g_own[s], g_sib[s]), info, chips)
-            g_last = pooled(done(g_last))
-        settle(pre, s - 2 if s > 2 else -1)
-        down(s, s < tensor - 1)
-        settle(pre if s == 1 else act, 0 if s == 1 else tensor - 1 if s == 2 else -1)
+    for s in range(1, end):
+        g_ahead = arrive(g_own, g_sib, g_ahead)
+        settle(("share", s - 1), ("x", end) if s > 1 else None, ("g", s - 2))
+        down(s)
+        settle(("g", 0))
         share(s)
+
+    settle(("g", end - 2))
+    first_share = done(add(*after(*shares[1])))
+    arrive(g_own, g_sib, g_ahead, False)
+    running = onward(lax.optimization_barrier((first_share, g_own[end]))[0])
+    columns = done(partner_columns(*after(g_own[end], g_sib[end]), info, chips))
+    pools["columns"] = pooled(columns)
+    g_there.append((pools["columns"], 0))
+    settle(("g", end - 1), ("share", end - 1))
+    down(end, False)
+    share(end)
 
     span = d // dp
     near, mine_j = pool_bit(chip, core), other_bits(chip, core)
-    g_there = [(theirs, hidden) for _, theirs in pre[:-1]] + [(g_last, 0)]
-    x_there = [(theirs, hidden) for _, theirs in act]
-    sums = {"down": (list(zip(g_own, g_sib)), g_there, act), "up": (list(zip(x_own, x_sib)), x_there, pre)}
-
-    def part(key, r):
+
+    def part(r, rows, there, rights):
         j = mine_j ^ r
-        at = chip_with(j, near, core)
-        straight, crossed = weight_part(*sums[key], at, j, core, 2 * span, hidden)
+        rows = [after(rows[0]), *rows[1:]]
+        straight, crossed = weight_part(rows, there, rights, chip_with(j, near, core), j, core, 2 * span, hidden)
+        done(straight)
         return [straight, crossed]
 
     bits = (chips // 2).bit_length() - 1
-    halves = {key: {} for key in sums}
-    for key in sums:
-        for r in reversed(range(1, chips // 2)):
-            halves[key][r] = part(key, r)
-    for s in range(2, tensor):
-        running = onward(add(*shares[s], running))
-    input_grad = add(*shares[0], running).reshape(OWNB, here, d)
-    for key in sums:
-        halves[key][0] = part(key, 0)
-
-    def finished(parts):
+
+    def pass_on(parts):
         for k in reversed(range(1, bits)):
             perm = chip_perm(dp, lambda c: 2 << k)
             for r in range(1 << k, 2 << k):
                 for h in range(2):
-                    parts[r ^ (1 << k)][h] = add(parts[r ^ (1 << k)][h], lax.ppermute(parts[r][h], "dp", perm))
+                    sent = lax.ppermute(parts[r][h], "dp", perm)
+                    kept = parts.get(r ^ (1 << k))
+                    parts[r ^ (1 << k)] = kept or [None, None]
+                    parts[r ^ (1 << k)][h] = add(kept[h], sent) if kept and kept[h] is not None else sent
         flip = lambda c: 2 >> c
         straight = lax.ppermute(parts[1][0], "dp", chip_perm(dp, flip))
         crossed = lax.ppermute(parts[1][1], "dp", chip_perm(dp, flip, True))
-        mine = add(parts[0][0], straight)
-        other = add(sibling(parts[0][1]), crossed)
-        return jnp.where(
+        return straight, crossed
+
+    def finished(kept, parts, straight, crossed):
+        extra = parts.get(0, [])
+        mine = add(kept[0], straight, *extra[:1])
+        other = add(sibling(add(kept[1], *extra[1:]) if extra else kept[1]), crossed)
+        return done(jnp.where(
             core == 0, jnp.concatenate([mine, other], axis=1), jnp.concatenate([other, mine], axis=1)
-        )
-
-    down_grad = finished(halves["down"])
-    up_grad = finished(halves["up"])
+        ))
+
+    down_sum, up_sum = (g_rows_of, g_there, act), (x_rows_of, x_there, pre)
+    away = list(reversed(range(1, chips // 2)))
+    settle("columns")
+    down_parts = {r: part(r, *down_sum) for r in away}
+    down_sent = pass_on(down_parts)
+    for s in range(2, end):
+        running = onward(done(add(*after(*shares[s]), running)))
+    settle(("g", end), ("share", end))
+    up_parts = {r: part(r, *up_sum) for r in away}
+    up_sent = pass_on(up_parts)
+    last.extend(down_sent)
+    down_kept = part(0, *down_sum)
+    running = onward(done(add(*after(*shares[end]), running)))
+    down_grad = finished(down_kept, down_parts, *down_sent)
+    up_kept = part(0, *up_sum)
+    input_grad = add(*shares[0], running).reshape(OWNB, here, d)
+    up_grad = finished(up_kept, up_parts, *up_sent)
     return input_grad, up_grad, down_grad
 
 

time: 419 us -> 281 us (0.67)
  Pallas kernels: 253 us -> 159 us
  waiting for transfers between devices: 96.9 us -> 67 us
  blocking collectives: 26.3 us -> 0 us
  starting transfers between devices: 20.3 us -> 29.3 us
    pallas_call x5 -> x6, Pallas kernels: 147 us -> 53.1 us  [the longest x4 46.4 us: weight_part(): pl.pallas_call(functools.partial(weight_body, begins=[begin for _, begin...]
    all_to_all x1 -> x0, blocking collectives: 26.3 us -> none  [exchange(): return lax.all_to_all(rows, 'dp', split_axis=0, concat_axis=0, tiled=True)]
    ppermute x9, waiting for transfers between devices: 44 us -> 23.3 us  [onward(): return lax.ppermute(piece, 'tensor', ring)]
    ppermute x9, waiting for transfers between devices: 24.7 us -> 5.69 us  [pooled(): return lax.ppermute(piece, 'dp', to_pool)]
    all_to_all x1 -> x2, waiting for transfers between devices: 0.01 us -> 17.7 us  [exchange(): return lax.all_to_all(rows, 'dp', split_axis=0, concat_axis=0, tiled=True)]
    ppermute x4, waiting for transfers between devices: 20.5 us -> 8.39 us  [the longest x2 8.38 us: pass_on(): crossed = lax.ppermute(parts[1][1], 'dp', chip_perm(dp, flip, True))]
    all_to_all x1 -> x2, starting transfers between devices: 4.3 us -> 9.48 us  [exchange(): return lax.all_to_all(rows, 'dp', split_axis=0, concat_axis=0, tiled=True)]
  transfers between devices with their start and end apart: 37 -> 38, of which waited for: 16 -> 17; matrix products, arithmetic and copies ran while one was open for 3% -> 5% of each run, Pallas kernels for 36% -> 54%
where the time goes in v2:
time: 281 us; the launch traced here: 280 us
  Pallas kernels  159 us (57%)
  waiting for transfers between devices  67 us (24%)
  starting transfers between devices  29.3 us (10%)
  other arithmetic  17.5 us (6%)
  local copies, waits for them, and re-layouts  6.35 us (2%)
    pallas_call x8, Pallas kernels, forward(): pl.pallas_call(functools.partial(body, hidden=hidden, chips=chips), out_s...  64.3 us
    pallas_call x4, Pallas kernels, weight_part(): pl.pallas_call(functools.partial(weight_body, begins=[begin for _, begin...  46.4 us
    pallas_call x4, Pallas kernels, input_part(): pl.pallas_call(input_body, out_shape=(shape, shape), grid_spec=pltpu.Pref...  30.8 us
    ppermute x9, waiting for transfers between devices, onward(): return lax.ppermute(piece, 'tensor', ring)  23.3 us
    all_to_all x2, waiting for transfers between devices, exchange(): return lax.all_to_all(rows, 'dp', split_axis=0, concat_axis=0, tiled=True)  17.7 us
    convert_element_type x8, other arithmetic, add(): return sum((v.astype(F32) for v in values)).astype(BF16)  12.8 us
    ppermute x14, waiting for transfers between devices, sibling(): return lax.ppermute(piece, 'dp', to_sibling)  11.9 us
    all_to_all x2, starting transfers between devices, exchange(): return lax.all_to_all(rows, 'dp', split_axis=0, concat_axis=0, tiled=True)  9.48 us
  transfers between devices with their start and end apart: 38, of which 17 were waited for; matrix products, arithmetic and copies ran while one was open for 5% of the time, Pallas kernels for 54%

profile of v2, /device:TPU:0, one launch (start us, length us, event | category | flops | bytes accessed | tf_op | source)
XLA Modules:
  0.0 280.4 jit_solution(6929227284346758910)
XLA Ops:
  1.3 3.4 %shard_map.85 = bf16[8,32,3072]{2,1,0:T(8,128)(2,1)} custom-call(s32[2]{0:T(128)} %pad_add_fusion.info, s32[8]{0:T(128)} %count.7, bf16[8,32,3072]{2,1,0:T(8,128)(2,1)} %rows.1), custom_call_target="tpu_custom_call" | custom-call | flops 1 | bytes 1 | tf_op jit(solution)/shard_map/pallas_call | solution.py:63
  4.7 5.2 %all-to-all-start = ((bf16[8,32,3072]{2,1,0:T(8,128)(2,1)}), bf16[8,32,3072]{2,1,0:T(8,128)(2,1)S(1)}, u32[]{:S(2)}, u32[]{:S(2)}) async-start(bf16[8,32,3072]{2,1,0:T(8,128)(2,1)} %shard_map.85), calls=%async_computation | async-start | bytes 3145728 | tf_op jit(solution)/shard_map/all_to_all | solution.py:335
  9.8 3.4 %shard_map.86 = bf16[8,32,3072]{2,1,0:T(8,128)(2,1)} custom-call(s32[2]{0:T(128)} %pad_add_fusion.info, s32[8]{0:T(128)} %count.7, bf16[8,32,3072]{2,1,0:T(8,128)(2,1)} %rows.2), custom_call_target="tpu_custom_call" | custom-call | flops 1 | bytes 1 | tf_op jit(solution)/shard_map/pallas_call | solution.py:63
  13.2 17.7 %all-to-all-done.rows = bf16[8,32,3072]{2,1,0:T(8,128)(2,1)S(1)} async-done(((bf16[8,32,3072]{2,1,0:T(8,128)(2,1)}), bf16[8,32,3072]{2,1,0:T(8,128)(2,1)S(1)}, u32[]{:S(2)}, u32[]{:S(2)}) %all-to-all-start) | async-done | bytes 1572896 | tf_op jit(solution)/shard_map/all_to_all | solution.py:335
  32.0 4.1 %shard_map.87 = bf16[4,32,3072]{2,1,0:T(8,128)(2,1)} custom-call(s32[2]{0:T(128)} %pad_add_fusion.info, s32[8]{0:T(128)} %count.7, s32[8,8]{1,0:T(8,128)} %patches.3, bf16[8,32,3072]{2,1,0:T(8,128)(2,1)} %copy-done.6), custom_call_target="tpu_custom_call" | custom-call | flops 1 | bytes 1 | tf_op jit(solution)/shard_map/pallas_call | solution.py:89
  36.1 1.6 collective-permute-start
  37.7 4.3 %all-to-all-start.1 = ((bf16[8,32,3072]{2,1,0:T(8,128)(2,1)}), bf16[8,32,3072]{2,1,0:T(8,128)(2,1)}, u32[]{:S(2)}, u32[]{:S(2)}) async-start(bf16[8,32,3072]{2,1,0:T(8,128)(2,1)} %shard_map.86), calls=%async_computation.1 | async-start | bytes 3145728 | tf_op jit(solution)/shard_map/all_to_all | solution.py:335
  42.9 8.2 %shard_map.88 = (bf16[256,3072]{1,0:T(8,128)(2,1)}, bf16[256,3072]{1,0:T(8,128)(2,1)}, bf16[256,1536]{1,0:T(8,128)(2,1)}) custom-call(s32[2]{0:T(128)} %pad_add_fusion.info, bf16[128,3072]{1,0:T(8,128)(2,1)} %bitcast.15, bf16[128,3072]{1,0:T(8,128)(2,1)} %copy-done.15, bf16[3072,3072]{1,0:T(8,128)(2,1)} %w.23), custom_call_target="tpu_custom_call" | custom-call | flops 1 | bytes 1 | tf_op jit(solution)/shard_map/pallas_call | solution.py:202
  51.1 7.2 %collective-permute-done.own = bf16[128,3072]{1,0:T(8,128)(2,1)} collective-permute-done((bf16[128,3072]{1,0:T(8,128)(2,1)}, bf16[128,3072]{1,0:T(8,128)(2,1)}, u32[]{:S(2)}, u32[]{:S(2)}) %collective-permute-start) | collective-permute-done | bytes 786464 | tf_op jit(solution)/shard_map/ppermute | solution.py:338
  58.8 2.0 collective-permute-done.2.sib
  61.6 8.2 %shard_map.89 = (bf16[256,3072]{1,0:T(8,128)(2,1)}, bf16[256,3072]{1,0:T(8,128)(2,1)}, bf16[256,1536]{1,0:T(8,128)(2,1)}) custom-call(s32[2]{0:T(128)} %pad_add_fusion.info, bf16[128,3072]{1,0:T(8,128)(2,1)} %collective-permute-done.own, bf16[128,3072]{1,0:T(8,128)(2,1)} %copy-done.16, bf16[3072,3072]{1,0:T(8,128)(2,1)} %w.23), custom_call_target="tpu_custom_call" | custom-call | flops 1 | bytes 1 | tf_op jit(solution)/shard_map/pallas_call | solution.py:202
  70.3 4.1 %shard_map.90 = bf16[4,32,3072]{2,1,0:T(8,128)(2,1)} custom-call(s32[2]{0:T(128)} %pad_add_fusion.info, s32[8]{0:T(128)} %count.7, s32[8,8]{1,0:T(8,128)} %patches.3, bf16[8,32,3072]{2,1,0:T(8,128)(2,1)} %all-to-all-done.1.rows), custom_call_target="tpu_custom_call" | custom-call | flops 1 | bytes 1 | tf_op jit(solution)/shard_map/pallas_call | solution.py:89
  74.4 5.9 %collective-permute-done.4.own = bf16[128,3072]{1,0:T(8,128)(2,1)} collective-permute-done((bf16[128,3072]{1,0:T(8,128)(2,1)}, bf16[128,3072]{1,0:T(8,128)(2,1)}, u32[]{:S(2)}, u32[]{:S(2)}) %collective-permute-start.4) | collective-permute-done | bytes 786464 | tf_op jit(solution)/shard_map/ppermute | solution.py:338
  80.8 2.1 collective-permute-done.5.sib
  82.9 8.2 %shard_map.91 = (bf16[256,3072]{1,0:T(8,128)(2,1)}, bf16[256,3072]{1,0:T(8,128)(2,1)}, bf16[256,1536]{1,0:T(8,128)(2,1)}) custom-call(s32[2]{0:T(128)} %pad_add_fusion.info, bf16[128,3072]{1,0:T(8,128)(2,1)} %collective-permute-done.4.own, bf16[128,3072]{1,0:T(8,128)(2,1)} %collective-permute-done.5.sib, bf16[3072,3072]{1,0:T(8,128)(2,1)} %w.23), custom_call_target="tpu_custom_call" | custom-call | flops 1 | bytes 1 | tf_op jit(solution)/shard_map/pallas_call | solution.py:202
  91.6 4.1 %collective-permute-done.7.refs_7_.refs_5_ = bf16[256,3072]{1,0:T(8,128)(2,1)S(1)} collective-permute-done((bf16[256,3072]{1,0:T(8,128)(2,1)}, bf16[256,3072]{1,0:T(8,128)(2,1)S(1)}, u32[]{:S(2)}, u32[]{:S(2)}) %collective-permute-start.7) | collective-permute-done | bytes 1572896 | tf_op jit(solution)/shard_map/ppermute | solution.py:344
  95.7 8.1 %shard_map.92 = (bf16[256,3072]{1,0:T(8,128)(2,1)}, bf16[256,3072]{1,0:T(8,128)(2,1)}) custom-call(s32[2]{0:T(128)} %pad_add_fusion.info, bf16[128,3072]{1,0:T(8,128)(2,1)} %bitcast.11, bf16[128,3072]{1,0:T(8,128)(2,1)} %collective-permute-done.3.sib, bf16[3072,3072]{1,0:T(8,128)(2,1)} %w.22, bf16[256,1536]{1,0:T(8,128)(2,1)} %get-tuple-element.100.slope), custom_call_target="tpu_custom_call" | custom-call | flops 1 | bytes 1 | tf_op jit(solution)/shard_map/pallas_call | solution.py:202
  105.0 1.6 collective-permute-start.12
  107.3 8.2 %shard_map.93 = (bf16[256,3072]{1,0:T(8,128)(2,1)}, bf16[256,3072]{1,0:T(8,128)(2,1)}, bf16[256,1536]{1,0:T(8,128)(2,1)}) custom-call(s32[2]{0:T(128)} %pad_add_fusion.info, bf16[128,3072]{1,0:T(8,128)(2,1)} %collective-permute-done.8.own, bf16[128,3072]{1,0:T(8,128)(2,1)} %collective-permute-done.9.sib, bf16[3072,3072]{1,0:T(8,128)(2,1)} %w.23), custom_call_target="tpu_custom_call" | custom-call | flops 1 | bytes 1 | tf_op jit(solution)/shard_map/pallas_call | solution.py:202
  115.5 7.7 %shard_map.94 = (bf16[128,3072]{1,0:T(8,128)(2,1)}, bf16[128,3072]{1,0:T(8,128)(2,1)}) custom-call(s32[2]{0:T(128)} %pad_add_fusion.info, bf16[256,3072]{1,0:T(8,128)(2,1)} %get-tuple-element.106.pre.refs_2_, bf16[3072,3072]{1,0:T(8,128)(2,1)} %w.23), custom_call_target="tpu_custom_call" | custom-call | flops 1 | bytes 1 | tf_op jit(solution)/shard_map/pallas_call | solution.py:229
  123.1 3.5 %collective-permute-done.12.own = bf16[128,3072]{1,0:T(8,128)(2,1)} collective-permute-done((bf16[128,3072]{1,0:T(8,128)(2,1)}, bf16[128,3072]{1,0:T(8,128)(2,1)}, u32[]{:S(2)}, u32[]{:S(2)}) %collective-permute-start.12) | collective-permute-done | bytes 786464 | tf_op jit(solution)/shard_map/ppermute | solution.py:338
  127.7 2.6 collective-permute-done.14.sib
  131.1 8.0 %shard_map.95 = (bf16[256,3072]{1,0:T(8,128)(2,1)}, bf16[256,3072]{1,0:T(8,128)(2,1)}) custom-call(s32[2]{0:T(128)} %pad_add_fusion.info, bf16[128,3072]{1,0:T(8,128)(2,1)} %collective-permute-done.12.own, bf16[128,3072]{1,0:T(8,128)(2,1)} %copy-done.13, bf16[3072,3072]{1,0:T(8,128)(2,1)} %w.22, bf16[256,1536]{1,0:T(8,128)(2,1)} %get-tuple-element.113.slope), custom_call_target="tpu_custom_call" | custom-call | flops 1 | bytes 1 | tf_op jit(solution)/shard_map/pallas_call | solution.py:202
  139.6 7.7 %shard_map.96 = (bf16[128,3072]{1,0:T(8,128)(2,1)}, bf16[128,3072]{1,0:T(8,128)(2,1)}) custom-call(s32[2]{0:T(128)} %pad_add_fusion.info, bf16[256,3072]{1,0:T(8,128)(2,1)} %get-tuple-element.115.pre.refs_6_, bf16[3072,3072]{1,0:T(8,128)(2,1)} %w.23), custom_call_target="tpu_custom_call" | custom-call | flops 1 | bytes 1 | tf_op jit(solution)/shard_map/pallas_call | solution.py:229
  147.3 1.4 collective-permute-done.13.own
  149.2 2.0 collective-permute-done.18.sib
  152.4 8.2 %shard_map.97 = (bf16[256,3072]{1,0:T(8,128)(2,1)}, bf16[256,3072]{1,0:T(8,128)(2,1)}) custom-call(s32[2]{0:T(128)} %pad_add_fusion.info, bf16[128,3072]{1,0:T(8,128)(2,1)} %collective-permute-done.13.own, bf16[128,3072]{1,0:T(8,128)(2,1)} %copy-done.14, bf16[3072,3072]{1,0:T(8,128)(2,1)} %w.22, bf16[256,1536]{1,0:T(8,128)(2,1)} %get-tuple-element.121.slope), custom_call_target="tpu_custom_call" | custom-call | flops 1 | bytes 1 | tf_op jit(solution)/shard_map/pallas_call | solution.py:202
  161.1 7.7 %shard_map.98 = (bf16[128,3072]{1,0:T(8,128)(2,1)}, bf16[128,3072]{1,0:T(8,128)(2,1)}) custom-call(s32[2]{0:T(128)} %pad_add_fusion.info, bf16[256,3072]{1,0:T(8,128)(2,1)} %get-tuple-element.123.pre.refs_10_, bf16[3072,3072]{1,0:T(8,128)(2,1)} %w.23), custom_call_target="tpu_custom_call" | custom-call | flops 1 | bytes 1 | tf_op jit(solution)/shard_map/pallas_call | solution.py:229
  168.8 2.2 add_convert_fusion.7
  171.5 1.8 collective-permute-done.21.sib
  174.2 3.1 %shard_map.99 = bf16[256,1536]{1,0:T(8,128)(2,1)} custom-call(s32[2]{0:T(128)} %pad_add_fusion.info, bf16[128,3072]{1,0:T(8,128)(2,1)} %copy-done.8, bf16[128,3072]{1,0:T(8,128)(2,1)} %copy-done.9), custom_call_target="tpu_custom_call" | custom-call | flops 1 | bytes 1 | tf_op jit(solution)/shard_map/pallas_call | solution.py:163
  177.3 1.9 collective-permute-start.25
  179.9 1.6 collective-permute-done.22.refs_9_.refs_11_
  181.5 7.4 %shard_map.100 = (bf16[256,1536]{1,0:T(8,128)(2,1)}, bf16[256,3072]{1,0:T(8,128)(2,1)}) custom-call(s32[2]{0:T(128)} %pad_add_fusion.info, bf16[128,3072]{1,0:T(8,128)(2,1)} %copy-done.8, bf16[128,3072]{1,0:T(8,128)(2,1)} %copy-done.9, bf16[3072,3072]{1,0:T(8,128)(2,1)} %w.22, bf16[256,1536]{1,0:T(8,128)(2,1)} %get-tuple-element.132.slope), custom_call_target="tpu_custom_call" | custom-call | flops 1 | bytes 1 | tf_op jit(solution)/shard_map/pallas_call | solution.py:202
  189.4 7.7 %shard_map.101 = (bf16[128,3072]{1,0:T(8,128)(2,1)}, bf16[128,3072]{1,0:T(8,128)(2,1)}) custom-call(s32[2]{0:T(128)} %pad_add_fusion.info, bf16[256,1536]{1,0:T(8,128)(2,1)} %get-tuple-element.134.pre.refs_14_, bf16[3072,3072]{1,0:T(8,128)(2,1)} %w.23), custom_call_target="tpu_custom_call" | custom-call | flops 1 | bytes 1 | tf_op jit(solution)/shard_map/pallas_call | solution.py:229
  198.0 11.7 %shard_map.102 = (bf16[384,1536]{1,0:T(8,128)(2,1)}, bf16[384,1536]{1,0:T(8,128)(2,1)}) custom-call(s32[3]{0:T(128)} %get-tuple-element.164.at, bf16[256,3072]{1,0:T(8,128)(2,1)} %get-tuple-element.154.refs_0_, bf16[256,3072]{1,0:T(8,128)(2,1)} %copy-done.3, bf16[256,3072]{1,0:T(8,128)(2,1)} %get-tuple-element.88.refs_2_, bf16[256,3072]{1,0:T(8,128)(2,1)} %copy-done, ...), custom_call_target="tpu_custom_call" | custom-call | flops 1 | bytes 1 | tf_op jit(solution)/shard_map/pallas_call | solution.py:289
  211.9 2.6 add_convert_fusion.6
  214.5 1.4 collective-permute-start.30
  216.8 11.5 %shard_map.103 = (bf16[384,1536]{1,0:T(8,128)(2,1)}, bf16[384,1536]{1,0:T(8,128)(2,1)}) custom-call(s32[3]{0:T(128)} %get-tuple-element.164.at, bf16[256,3072]{1,0:T(8,128)(2,1)} %get-tuple-element.159.refs_0_, bf16[256,3072]{1,0:T(8,128)(2,1)} %copy-done, bf16[256,3072]{1,0:T(8,128)(2,1)} %get-tuple-element.106.pre.refs_2_, bf16[256,3072]{1,0:T(8,128)(2,1)} %copy-done.3, ...), custom_call_target="tpu_custom_call" | custom-call | flops 1 | bytes 1 | tf_op jit(solution)/shard_map/pallas_call | solution.py:289
  230.0 8.4 %collective-permute-done.29 = bf16[384,1536]{1,0:T(8,128)(2,1)S(1)} collective-permute-done((bf16[384,1536]{1,0:T(8,128)(2,1)}, bf16[384,1536]{1,0:T(8,128)(2,1)S(1)}, u32[]{:S(2)}, u32[]{:S(2)}) %collective-permute-start.29) | collective-permute-done | bytes 1179680 | tf_op jit(solution)/shard_map/ppermute | solution.py:447
  238.4 11.6 %shard_map.104 = (bf16[384,1536]{1,0:T(8,128)(2,1)}, bf16[384,1536]{1,0:T(8,128)(2,1)}) custom-call(s32[3]{0:T(128)} %get-tuple-element.163.at, bf16[256,3072]{1,0:T(8,128)(2,1)} %get-tuple-element.154.refs_0_, bf16[256,3072]{1,0:T(8,128)(2,1)} %copy-done.3, bf16[256,3072]{1,0:T(8,128)(2,1)} %get-tuple-element.88.refs_2_, bf16[256,3072]{1,0:T(8,128)(2,1)} %copy-done, ...), custom_call_target="tpu_custom_call" | custom-call | flops 1 | bytes 1 | tf_op jit(solution)/shard_map/pallas_call | solution.py:289
  250.6 2.8 %add_convert_fusion.5 = bf16[128,3072]{1,0:T(8,128)(2,1)} fusion(bf16[128,3072]{1,0:T(8,128)(2,1)} %collective-permute-done.30, bf16[128,3072]{1,0:T(8,128)(2,1)} %collective-permute-done.24, bf16[128,3072]{1,0:T(8,128)(2,1)} %get-tuple-element.156), kind=kLoop, calls=%fused_computation.7 | loop fusion | flops 2359296 | bytes 3145728 | tf_op jit(solution)/shard_map/convert_element_type | solution.py:310
  254.8 1.6 add_convert_fusion.3
  256.6 1.7 maximum_select_fusion
  258.3 11.7 %shard_map.105 = (bf16[384,1536]{1,0:T(8,128)(2,1)}, bf16[384,1536]{1,0:T(8,128)(2,1)}) custom-call(s32[3]{0:T(128)} %get-tuple-element.163.at, bf16[256,3072]{1,0:T(8,128)(2,1)} %get-tuple-element.159.refs_0_, bf16[256,3072]{1,0:T(8,128)(2,1)} %copy-done, bf16[256,3072]{1,0:T(8,128)(2,1)} %get-tuple-element.106.pre.refs_2_, bf16[256,3072]{1,0:T(8,128)(2,1)} %copy-done.3, ...), custom_call_target="tpu_custom_call" | custom-call | flops 1 | bytes 1 | tf_op jit(solution)/shard_map/pallas_call | solution.py:289
  270.1 5.3 %collective-permute-done.31 = bf16[128,3072]{1,0:T(8,128)(2,1)} collective-permute-done((bf16[128,3072]{1,0:T(8,128)(2,1)}, bf16[128,3072]{1,0:T(8,128)(2,1)}, u32[]{:S(2)}, u32[]{:S(2)}) %collective-permute-start.31) | collective-permute-done | bytes 786464 | tf_op jit(solution)/shard_map/ppermute | solution.py:338
  275.4 2.7 add_convert_fusion.4
  278.7 1.7 maximum_select_fusion.1
  (103 shorter events, 23.3 us)
Async XLA Ops:
  4.7 26.2 %all-to-all-start = ((bf16[8,32,3072]{2,1,0:T(8,128)(2,1)}), bf16[8,32,3072]{2,1,0:T(8,128)(2,1)S(1)}, u32[]{:S(2)}, u32[]{:S(2)}) async-start(bf16[8,32,3072]{2,1,0:T(8,128)(2,1)} %shard_map.85), calls=%async_computation | async-start | bytes 3145728 | tf_op jit(solution)/shard_map/all_to_all | solution.py:335
  36.1 5.9 %collective-permute-start.1 = (bf16[128,3072]{1,0:T(8,128)(2,1)}, bf16[128,3072]{1,0:T(8,128)(2,1)S(1)}, u32[]{:S(2)}, u32[]{:S(2)}) collective-permute-start(bf16[128,3072]{1,0:T(8,128)(2,1)} %bitcast.13), channel_id=1, source_target_pairs={{0,4},{4,0},{8,12},{12,8},{16,20},{20,16},{24,28},{28,24},{1,5},{5... | collective-permute-start | bytes 2359304 | tf_op jit(solution)/shard_map/ppermute | solution.py:341
  36.1 22.1 %collective-permute-start = (bf16[128,3072]{1,0:T(8,128)(2,1)}, bf16[128,3072]{1,0:T(8,128)(2,1)}, u32[]{:S(2)}, u32[]{:S(2)}) collective-permute-start(bf16[128,3072]{1,0:T(8,128)(2,1)} %bitcast.14), channel_id=1, source_target_pairs={{0,1},{1,2},{2,3},{3,0},{4,5},{5,6},{6,7},{7,4},{8,9},{9,10},{10,1... | collective-permute-start | bytes 2359304 | tf_op jit(solution)/shard_map/ppermute | solution.py:338
  37.7 32.6 %all-to-all-start.1 = ((bf16[8,32,3072]{2,1,0:T(8,128)(2,1)}), bf16[8,32,3072]{2,1,0:T(8,128)(2,1)}, u32[]{:S(2)}, u32[]{:S(2)}) async-start(bf16[8,32,3072]{2,1,0:T(8,128)(2,1)} %shard_map.86), calls=%async_computation.1 | async-start | bytes 3145728 | tf_op jit(solution)/shard_map/all_to_all | solution.py:335
  58.2 2.5 collective-permute-start.2
  58.2 22.1 %collective-permute-start.4 = (bf16[128,3072]{1,0:T(8,128)(2,1)}, bf16[128,3072]{1,0:T(8,128)(2,1)}, u32[]{:S(2)}, u32[]{:S(2)}) collective-permute-start(bf16[128,3072]{1,0:T(8,128)(2,1)} %collective-permute-done.own), channel_id=1, source_target_pairs={{0,1},{1,2},{2,3},{3,0},{4,5},{5,6},{6,7},{7,4},{8,9},{9,10},{10,1... | collective-permute-start | bytes 2359304 | tf_op jit(solution)/shard_map/ppermute | solution.py:338
  58.3 22.6 %collective-permute-start.6 = (bf16[256,3072]{1,0:T(8,128)(2,1)}, bf16[256,3072]{1,0:T(8,128)(2,1)S(1)}, u32[]{:S(2)}, u32[]{:S(2)}) collective-permute-start(bf16[256,3072]{1,0:T(8,128)(2,1)} %get-tuple-element.88.refs_2_), channel_id=1, source_target_pairs={{0,8},{4,20},{8,0},{12,28},{16,24},{20,4},{24,16},{28,12},{1,9},{5... | collective-permute-start | bytes 4718600 | tf_op jit(solution)/shard_map/ppermute | solution.py:344
  69.8 25.9 %collective-permute-start.7 = (bf16[256,3072]{1,0:T(8,128)(2,1)}, bf16[256,3072]{1,0:T(8,128)(2,1)S(1)}, u32[]{:S(2)}, u32[]{:S(2)}) collective-permute-start(bf16[256,3072]{1,0:T(8,128)(2,1)} %get-tuple-element.92.refs_6_), channel_id=1, source_target_pairs={{0,8},{4,20},{8,0},{12,28},{16,24},{20,4},{24,16},{28,12},{1,9},{5... | collective-permute-start | bytes 4718600 | tf_op jit(solution)/shard_map/ppermute | solution.py:344
  80.3 2.6 collective-permute-start.5
  80.3 11.3 %collective-permute-start.3 = (bf16[128,3072]{1,0:T(8,128)(2,1)}, bf16[128,3072]{1,0:T(8,128)(2,1)}, u32[]{:S(2)}, u32[]{:S(2)}) collective-permute-start(bf16[128,3072]{1,0:T(8,128)(2,1)} %bitcast.10), channel_id=1, source_target_pairs={{0,4},{4,0},{8,12},{12,8},{16,20},{20,16},{24,28},{28,24},{1,5},{5... | collective-permute-start | bytes 2359304 | tf_op jit(solution)/shard_map/ppermute | solution.py:341
  80.8 23.0 %collective-permute-start.8 = (bf16[128,3072]{1,0:T(8,128)(2,1)}, bf16[128,3072]{1,0:T(8,128)(2,1)}, u32[]{:S(2)}, u32[]{:S(2)}) collective-permute-start(bf16[128,3072]{1,0:T(8,128)(2,1)} %collective-permute-done.4.own), channel_id=1, source_target_pairs={{0,1},{1,2},{2,3},{3,0},{4,5},{5,6},{6,7},{7,4},{8,9},{9,10},{10,1... | collective-permute-start | bytes 2359304 | tf_op jit(solution)/shard_map/ppermute | solution.py:338
  80.8 10.3 %copy-start = (bf16[256,3072]{1,0:T(8,128)(2,1)}, bf16[256,3072]{1,0:T(8,128)(2,1)S(1)}, u32[]{:S(2)}) copy-start(bf16[256,3072]{1,0:T(8,128)(2,1)S(1)} %collective-permute-done.6.refs_3_.refs_1_) | copy-start | bytes 4718596
  91.1 24.4 %collective-permute-start.10 = (bf16[256,3072]{1,0:T(8,128)(2,1)}, bf16[256,3072]{1,0:T(8,128)(2,1)S(1)}, u32[]{:S(2)}, u32[]{:S(2)}) collective-permute-start(bf16[256,3072]{1,0:T(8,128)(2,1)} %get-tuple-element.97.refs_10_), channel_id=1, source_target_pairs={{0,8},{4,20},{8,0},{12,28},{16,24},{20,4},{24,16},{28,12},{1,9},{5... | collective-permute-start | bytes 4718600 | tf_op jit(solution)/shard_map/ppermute | solution.py:344
  95.7 8.1 %copy-start.1 = (bf16[256,3072]{1,0:T(8,128)(2,1)}, bf16[256,3072]{1,0:T(8,128)(2,1)S(1)}, u32[]{:S(2)}) copy-start(bf16[256,3072]{1,0:T(8,128)(2,1)S(1)} %collective-permute-done.7.refs_7_.refs_5_) | copy-start | bytes 4718596
  103.9 3.4 %collective-permute-start.9 = (bf16[128,3072]{1,0:T(8,128)(2,1)}, bf16[128,3072]{1,0:T(8,128)(2,1)}, u32[]{:S(2)}, u32[]{:S(2)}) collective-permute-start(bf16[128,3072]{1,0:T(8,128)(2,1)} %collective-permute-done.8.own), channel_id=1, source_target_pairs={{0,4},{4,0},{8,12},{12,8},{16,20},{20,16},{24,28},{28,24},{1,5},{5... | collective-permute-start | bytes 2359304 | tf_op jit(solution)/shard_map/ppermute | solution.py:341
  105.0 21.6 %collective-permute-start.12 = (bf16[128,3072]{1,0:T(8,128)(2,1)}, bf16[128,3072]{1,0:T(8,128)(2,1)}, u32[]{:S(2)}, u32[]{:S(2)}) collective-permute-start(bf16[128,3072]{1,0:T(8,128)(2,1)} %bitcast.12), channel_id=1, source_target_pairs={{0,1},{1,2},{2,3},{3,0},{4,5},{5,6},{6,7},{7,4},{8,9},{9,10},{10,1... | collective-permute-start | bytes 2359304 | tf_op jit(solution)/shard_map/ppermute | solution.py:338
  106.6 33.0 %collective-permute-start.15 = (bf16[256,3072]{1,0:T(8,128)(2,1)}, bf16[256,3072]{1,0:T(8,128)(2,1)S(1)}, u32[]{:S(2)}, u32[]{:S(2)}) collective-permute-start(bf16[256,3072]{1,0:T(8,128)(2,1)} %get-tuple-element.106.pre.refs_2_), channel_id=1, source_target_pairs={{0,8},{4,20},{8,0},{12,28},{16,24},{20,4},{24,16},{28,12},{1,9},{5... | collective-permute-start | bytes 4718600 | tf_op jit(solution)/shard_map/ppermute | solution.py:344
  115.5 7.7 %copy-start.2 = (bf16[256,3072]{1,0:T(8,128)(2,1)}, bf16[256,3072]{1,0:T(8,128)(2,1)S(1)}, u32[]{:S(2)}) copy-start(bf16[256,3072]{1,0:T(8,128)(2,1)S(1)} %collective-permute-done.10.refs_11_.refs_9_) | copy-start | bytes 4718596
  126.7 3.6 %collective-permute-start.14 = (bf16[128,3072]{1,0:T(8,128)(2,1)}, bf16[128,3072]{1,0:T(8,128)(2,1)S(1)}, u32[]{:S(2)}, u32[]{:S(2)}) collective-permute-start(bf16[128,3072]{1,0:T(8,128)(2,1)} %collective-permute-done.12.own), channel_id=1, source_target_pairs={{0,4},{4,0},{8,12},{12,8},{16,20},{20,16},{24,28},{28,24},{1,5},{5... | collective-permute-start | bytes 2359304 | tf_op jit(solution)/shard_map/ppermute | solution.py:341
  126.7 3.7 %collective-permute-start.11 = (bf16[128,3072]{1,0:T(8,128)(2,1)}, bf16[128,3072]{1,0:T(8,128)(2,1)}, u32[]{:S(2)}, u32[]{:S(2)}) collective-permute-start(bf16[128,3072]{1,0:T(8,128)(2,1)} %get-tuple-element.108), channel_id=1, source_target_pairs={{0,4},{4,0},{8,12},{12,8},{16,20},{20,16},{24,28},{28,24},{1,5},{5... | collective-permute-start | bytes 2359304 | tf_op jit(solution)/shard_map/ppermute | solution.py:341
  127.2 21.6 %collective-permute-start.13 = (bf16[128,3072]{1,0:T(8,128)(2,1)}, bf16[128,3072]{1,0:T(8,128)(2,1)}, u32[]{:S(2)}, u32[]{:S(2)}) collective-permute-start(bf16[128,3072]{1,0:T(8,128)(2,1)} %collective-permute-done.12.own), channel_id=1, source_target_pairs={{0,1},{1,2},{2,3},{3,0},{4,5},{5,6},{6,7},{7,4},{8,9},{9,10},{10,1... | collective-permute-start | bytes 2359304 | tf_op jit(solution)/shard_map/ppermute | solution.py:338
  127.2 25.2 %collective-permute-start.19 = (bf16[256,3072]{1,0:T(8,128)(2,1)}, bf16[256,3072]{1,0:T(8,128)(2,1)S(1)}, u32[]{:S(2)}, u32[]{:S(2)}) collective-permute-start(bf16[256,3072]{1,0:T(8,128)(2,1)} %get-tuple-element.105.refs_14_), channel_id=1, source_target_pairs={{0,8},{4,20},{8,0},{12,28},{16,24},{20,4},{24,16},{28,12},{1,9},{5... | collective-permute-start | bytes 4718600 | tf_op jit(solution)/shard_map/ppermute | solution.py:344
  139.1 29.7 %collective-permute-start.20 = (bf16[256,3072]{1,0:T(8,128)(2,1)}, bf16[256,3072]{1,0:T(8,128)(2,1)}, u32[]{:S(2)}, u32[]{:S(2)}) collective-permute-start(bf16[256,3072]{1,0:T(8,128)(2,1)} %get-tuple-element.115.pre.refs_6_), channel_id=1, source_target_pairs={{0,8},{4,20},{8,0},{12,28},{16,24},{20,4},{24,16},{28,12},{1,9},{5... | collective-permute-start | bytes 4718600 | tf_op jit(solution)/shard_map/ppermute | solution.py:344
  139.6 7.7 %copy-start.3 = (bf16[256,3072]{1,0:T(8,128)(2,1)}, bf16[256,3072]{1,0:T(8,128)(2,1)S(1)}, u32[]{:S(2)}) copy-start(bf16[256,3072]{1,0:T(8,128)(2,1)S(1)} %collective-permute-done.15.refs_1_.refs_3_) | copy-start | bytes 4718596
  148.7 2.5 collective-permute-start.18
  148.7 3.6 %collective-permute-start.17 = (bf16[128,3072]{1,0:T(8,128)(2,1)}, bf16[128,3072]{1,0:T(8,128)(2,1)S(1)}, u32[]{:S(2)}, u32[]{:S(2)}) collective-permute-start(bf16[128,3072]{1,0:T(8,128)(2,1)} %get-tuple-element.116), channel_id=1, source_target_pairs={{0,4},{4,0},{8,12},{12,8},{16,20},{20,16},{24,28},{28,24},{1,5},{5... | collective-permute-start | bytes 2359304 | tf_op jit(solution)/shard_map/ppermute | solution.py:341
  149.2 21.8 %collective-permute-start.16 = (bf16[128,3072]{1,0:T(8,128)(2,1)}, bf16[128,3072]{1,0:T(8,128)(2,1)S(1)}, u32[]{:S(2)}, u32[]{:S(2)}) collective-permute-start(bf16[128,3072]{1,0:T(8,128)(2,1)} %collective-permute-done.13.own), channel_id=1, source_target_pairs={{0,1},{1,2},{2,3},{3,0},{4,5},{5,6},{6,7},{7,4},{8,9},{9,10},{10,1... | collective-permute-start | bytes 2359304 | tf_op jit(solution)/shard_map/ppermute | solution.py:338
  152.3 8.2 %copy-start.20 = (bf16[128,3072]{1,0:T(8,128)(2,1)}, bf16[128,3072]{1,0:T(8,128)(2,1)S(1)}, u32[]{:S(2)}) copy-start(bf16[128,3072]{1,0:T(8,128)(2,1)S(1)} %collective-permute-done.17) | copy-start | bytes 2359300
  152.4 8.2 %copy-start.4 = (bf16[256,3072]{1,0:T(8,128)(2,1)}, bf16[256,3072]{1,0:T(8,128)(2,1)S(1)}, u32[]{:S(2)}) copy-start(bf16[256,3072]{1,0:T(8,128)(2,1)S(1)} %collective-permute-done.19.refs_15_.refs_13_) | copy-start | bytes 4718596
  160.5 8.3 %copy-start.19 = (bf16[128,3072]{1,0:T(8,128)(2,1)S(1)}, bf16[128,3072]{1,0:T(8,128)(2,1)}, u32[]{:S(2)}) copy-start(bf16[128,3072]{1,0:T(8,128)(2,1)} %get-tuple-element.125) | copy-start | bytes 2359300
  160.5 21.0 %collective-permute-start.22 = (bf16[256,3072]{1,0:T(8,128)(2,1)}, bf16[256,3072]{1,0:T(8,128)(2,1)S(1)}, u32[]{:S(2)}, u32[]{:S(2)}) collective-permute-start(bf16[256,3072]{1,0:T(8,128)(2,1)} %get-tuple-element.123.pre.refs_10_), channel_id=1, source_target_pairs={{0,8},{4,20},{8,0},{12,28},{16,24},{20,4},{24,16},{28,12},{1,9},{5... | collective-permute-start | bytes 4718600 | tf_op jit(solution)/shard_map/ppermute | solution.py:344
  171.0 2.3 collective-permute-start.21
  171.2 8.7 %collective-permute-start.23 = (bf16[128,3072]{1,0:T(8,128)(2,1)}, bf16[128,3072]{1,0:T(8,128)(2,1)}, u32[]{:S(2)}, u32[]{:S(2)}) collective-permute-start(bf16[128,3072]{1,0:T(8,128)(2,1)} %get-tuple-element.124), channel_id=1, source_target_pairs={{0,4},{4,0},{8,12},{12,8},{16,20},{20,16},{24,28},{28,24},{1,5},{5... | collective-permute-start | bytes 2359304 | tf_op jit(solution)/shard_map/ppermute | solution.py:341
  177.3 19.8 %collective-permute-start.25 = (bf16[256,1536]{1,0:T(8,128)(2,1)}, bf16[256,1536]{1,0:T(8,128)(2,1)S(1)}, u32[]{:S(2)}, u32[]{:S(2)}) collective-permute-start(bf16[256,1536]{1,0:T(8,128)(2,1)} %shard_map.99), channel_id=1, source_target_pairs={{0,8},{4,20},{8,0},{12,28},{16,24},{20,4},{24,16},{28,12},{1,9},{5... | collective-permute-start | bytes 2359304 | tf_op jit(solution)/shard_map/ppermute | solution.py:344
  179.3 32.7 %collective-permute-start.26 = (bf16[128,3072]{1,0:T(8,128)(2,1)}, bf16[128,3072]{1,0:T(8,128)(2,1)}, u32[]{:S(2)}, u32[]{:S(2)}) collective-permute-start(bf16[128,3072]{1,0:T(8,128)(2,1)} %add_convert_fusion.7), channel_id=1, source_target_pairs={{0,1},{1,2},{2,3},{3,0},{4,5},{5,6},{6,7},{7,4},{8,9},{9,10},{10,1... | collective-permute-start | bytes 2359304 | tf_op jit(solution)/shard_map/ppermute | solution.py:338
  181.5 7.4 %copy-start.5 = (bf16[256,3072]{1,0:T(8,128)(2,1)}, bf16[256,3072]{1,0:T(8,128)(2,1)S(1)}, u32[]{:S(2)}) copy-start(bf16[256,3072]{1,0:T(8,128)(2,1)S(1)} %collective-permute-done.22.refs_9_.refs_11_) | copy-start | bytes 4718596
  188.9 27.0 %collective-permute-start.27 = (bf16[256,1536]{1,0:T(8,128)(2,1)}, bf16[256,1536]{1,0:T(8,128)(2,1)S(1)}, u32[]{:S(2)}, u32[]{:S(2)}) collective-permute-start(bf16[256,1536]{1,0:T(8,128)(2,1)} %get-tuple-element.134.pre.refs_14_), channel_id=1, source_target_pairs={{0,8},{4,20},{8,0},{12,28},{16,24},{20,4},{24,16},{28,12},{1,9},{5... | collective-permute-start | bytes 2359304 | tf_op jit(solution)/shard_map/ppermute | solution.py:344
  197.1 18.8 %collective-permute-start.24 = (bf16[128,3072]{1,0:T(8,128)(2,1)}, bf16[128,3072]{1,0:T(8,128)(2,1)}, u32[]{:S(2)}, u32[]{:S(2)}) collective-permute-start(bf16[128,3072]{1,0:T(8,128)(2,1)} %get-tuple-element.136), channel_id=1, source_target_pairs={{0,4},{4,0},{8,12},{12,8},{16,20},{20,16},{24,28},{28,24},{1,5},{5... | collective-permute-start | bytes 2359304 | tf_op jit(solution)/shard_map/ppermute | solution.py:341
  198.0 13.9 %copy-start.18 = (bf16[128,3072]{1,0:T(8,128)(2,1)S(1)}, bf16[128,3072]{1,0:T(8,128)(2,1)}, u32[]{:S(2)}) copy-start(bf16[128,3072]{1,0:T(8,128)(2,1)} %get-tuple-element.145) | copy-start | bytes 2359300
  209.7 28.6 %collective-permute-start.28 = (bf16[384,1536]{1,0:T(8,128)(2,1)}, bf16[384,1536]{1,0:T(8,128)(2,1)}, u32[]{:S(2)}, u32[]{:S(2)}) collective-permute-start(bf16[384,1536]{1,0:T(8,128)(2,1)} %get-tuple-element.144), channel_id=1, source_target_pairs={{0,16},{4,12},{8,24},{12,4},{16,0},{20,28},{24,8},{28,20},{1,17},{... | collective-permute-start | bytes 3538952 | tf_op jit(solution)/shard_map/ppermute | solution.py:446
  210.7 27.7 %collective-permute-start.29 = (bf16[384,1536]{1,0:T(8,128)(2,1)}, bf16[384,1536]{1,0:T(8,128)(2,1)S(1)}, u32[]{:S(2)}, u32[]{:S(2)}) collective-permute-start(bf16[384,1536]{1,0:T(8,128)(2,1)} %get-tuple-element.153), channel_id=1, source_target_pairs={{0,20},{4,8},{8,28},{12,0},{16,4},{20,24},{24,12},{28,16},{1,21},{... | collective-permute-start | bytes 3538952 | tf_op jit(solution)/shard_map/ppermute | solution.py:447
  214.5 36.0 %collective-permute-start.30 = (bf16[128,3072]{1,0:T(8,128)(2,1)}, bf16[128,3072]{1,0:T(8,128)(2,1)}, u32[]{:S(2)}, u32[]{:S(2)}) collective-permute-start(bf16[128,3072]{1,0:T(8,128)(2,1)} %add_convert_fusion.6), channel_id=1, source_target_pairs={{0,1},{1,2},{2,3},{3,0},{4,5},{5,6},{6,7},{7,4},{8,9},{9,10},{10,1... | collective-permute-start | bytes 2359304 | tf_op jit(solution)/shard_map/ppermute | solution.py:338
  228.3 50.1 %collective-permute-start.35 = (bf16[384,1536]{1,0:T(8,128)(2,1)}, bf16[384,1536]{1,0:T(8,128)(2,1)S(1)}, u32[]{:S(2)}, u32[]{:S(2)}) collective-permute-start(bf16[384,1536]{1,0:T(8,128)(2,1)} %get-tuple-element.162), channel_id=1, source_target_pairs={{0,20},{4,8},{8,28},{12,0},{16,4},{20,24},{24,12},{28,16},{1,21},{... | collective-permute-start | bytes 3538952 | tf_op jit(solution)/shard_map/ppermute | solution.py:447
  229.2 48.9 %collective-permute-start.33 = (bf16[384,1536]{1,0:T(8,128)(2,1)}, bf16[384,1536]{1,0:T(8,128)(2,1)S(1)}, u32[]{:S(2)}, u32[]{:S(2)}) collective-permute-start(bf16[384,1536]{1,0:T(8,128)(2,1)} %get-tuple-element.152), channel_id=1, source_target_pairs={{0,16},{4,12},{8,24},{12,4},{16,0},{20,28},{24,8},{28,20},{1,17},{... | collective-permute-start | bytes 3538952 | tf_op jit(solution)/shard_map/ppermute | solution.py:446
  249.9 6.4 %collective-permute-start.32 = (bf16[384,1536]{1,0:T(8,128)(2,1)}, bf16[384,1536]{1,0:T(8,128)(2,1)S(1)}, u32[]{:S(2)}, u32[]{:S(2)}) collective-permute-start(bf16[384,1536]{1,0:T(8,128)(2,1)} %get-tuple-element.158), channel_id=1, source_target_pairs={{0,4},{4,0},{8,12},{12,8},{16,20},{20,16},{24,28},{28,24},{1,5},{5... | collective-permute-start | bytes 3538952 | tf_op jit(solution)/shard_map/ppermute | solution.py:341
  253.4 21.9 %collective-permute-start.31 = (bf16[128,3072]{1,0:T(8,128)(2,1)}, bf16[128,3072]{1,0:T(8,128)(2,1)}, u32[]{:S(2)}, u32[]{:S(2)}) collective-permute-start(bf16[128,3072]{1,0:T(8,128)(2,1)} %add_convert_fusion.5), channel_id=1, source_target_pairs={{0,1},{1,2},{2,3},{3,0},{4,5},{5,6},{6,7},{7,4},{8,9},{9,10},{10,1... | collective-permute-start | bytes 2359304 | tf_op jit(solution)/shard_map/ppermute | solution.py:338
  258.3 17.1 %copy-start.17 = (bf16[128,3072]{1,0:T(8,128)(2,1)S(1)}, bf16[128,3072]{1,0:T(8,128)(2,1)}, u32[]{:S(2)}) copy-start(bf16[128,3072]{1,0:T(8,128)(2,1)} %get-tuple-element.107) | copy-start | bytes 2359300
  270.0 8.4 %collective-permute-start.34 = (bf16[384,1536]{1,0:T(8,128)(2,1)}, bf16[384,1536]{1,0:T(8,128)(2,1)S(1)}, u32[]{:S(2)}, u32[]{:S(2)}) collective-permute-start(bf16[384,1536]{1,0:T(8,128)(2,1)} %get-tuple-element.161), channel_id=1, source_target_pairs={{0,4},{4,0},{8,12},{12,8},{16,20},{20,16},{24,28},{28,24},{1,5},{5... | collective-permute-start | bytes 3538952 | tf_op jit(solution)/shard_map/ppermute | solution.py:341
  (11 other events, 17.5 us)
